TPU v7x, 256 devices: a whole 4x4x8 slice. The times are simulated.
256 devices in a mesh: dp: 32 (over z_lo, y, x), ctx: 8 (over z_hi, core).
Axes of the slice: x: 4, y: 4, z: 8 (z_hi: 4, z_lo: 2; z = z_hi * 2 + z_lo), core: 2. Of those that a mesh axis runs over, the one named last changes fastest.
Arguments:
- inputs: bfloat16 [32768, 1024], P(('dp', 'ctx')), may hold values from -6 to 6
- input_weight: bfloat16 [1024, 4096], P('dp'), may hold values from -0.1875 to 0.1875
- output_weight: bfloat16 [1024, 1024], P('dp'), may hold values from -0.1875 to 0.1875
- cotangent: bfloat16 [32768, 1024], P(('dp', 'ctx')), may hold values from -6 to 6
- lengths: int32 [32, 4], P('dp'), may hold values from 1 to 768, 1024 in all within a row
- buckets: int32 [1024], replicated, may hold values from 0 to 31
- bias_weights: float32 [8, 32], replicated, may hold values from -4 to 4
Outputs:
- outputs: bfloat16 [32768, 1024], P(('dp', 'ctx'))
- input_grads: bfloat16 [32768, 1024], P(('dp', 'ctx'))
- weight_grads: float32 [1024, 1024], P('dp', 'ctx')
Inputs may be any that keep to these rules, and one draw needn't show every extreme that they name: Each row holds the 4 history lengths of one group, summing to 1024; the longest is exactly 768.
All inputs are finite; a program needn't handle non-finite values.
Results may differ from a plain program's by a relative error of at most 0.034.
Values may be sent and summed in bfloat16 or wider, within the bound.
A program may use at most 256 MiB of HBM per device.

v0:
```python
import math

import jax
import jax.numpy as jnp
from jax import lax
from jax.sharding import PartitionSpec as P

EPSILON = 1e-06


def silu_grad(values):
    sigmoid = jax.nn.sigmoid(values)
    return sigmoid * (1.0 + values * (1.0 - sigmoid))


def normalize(values):
    average = jnp.mean(values, axis=-1, keepdims=True)
    centered = values - average
    inverse = lax.rsqrt(jnp.mean(centered * centered, axis=-1, keepdims=True) + EPSILON)
    return (centered * inverse, inverse)


def normalize_back(normed, inverse, upstream):
    first = jnp.mean(upstream, axis=-1, keepdims=True)
    second = jnp.mean(upstream * normed, axis=-1, keepdims=True)
    return (upstream - first - normed * second) * inverse


def segment_of(positions, boundary):
    return jnp.sum((positions[:, None] >= boundary[None, :]).astype(jnp.int32), axis=1)


def mask_block(query_pos, key_pos, boundary):
    shared = segment_of(query_pos, boundary)[:, None] == segment_of(key_pos, boundary)[None, :]
    return shared & (key_pos[None, :] <= query_pos[:, None])


def score_block(query_block, key_block, bias_slice, scale):
    products = jnp.einsum(
        "rhd,khd->hrk", query_block, key_block, preferred_element_type=jnp.float32
    )
    return products * scale + bias_slice


def attention_pair(
    query_block, key_block, value_block, grad_block, bias_slice, scale, seq, allowed
):
    scores = score_block(query_block, key_block, bias_slice, scale)
    weights = jnp.where(allowed[None], jax.nn.silu(scores) / seq, 0.0).astype(jnp.bfloat16)
    d_weights = jnp.einsum(
        "rhd,khd->hrk", grad_block, value_block, preferred_element_type=jnp.float32
    )
    d_scores = jnp.where(allowed[None], d_weights * silu_grad(scores) / seq, 0.0).astype(
        jnp.bfloat16
    )
    return (weights, d_scores)


def on_device(inputs, input_weight, output_weight, cotangent, lengths, buckets, bias_weights):
    rows, width = inputs.shape
    seq = rows * lax.axis_size("ctx")
    heads = bias_weights.shape[0]
    head_size = width // heads
    scale = 1.0 / math.sqrt(head_size)
    block = min(512, seq)
    full_in, full_out = (
        lax.all_gather(input_weight, "dp", axis=0, tiled=True),
        lax.all_gather(output_weight, "dp", axis=0, tiled=True),
    )
    bias_table = bias_weights[:, buckets]
    boundary = jnp.cumsum(lengths[0])
    own_pos = lax.axis_index("ctx") * rows + jnp.arange(rows, dtype=jnp.int32)
    all_pos = jnp.arange(seq, dtype=jnp.int32)
    own_bias = jnp.take(bias_table, jnp.maximum(own_pos[:, None] - all_pos[None, :], 0), axis=1)
    normed_x, inverse_x = normalize(inputs.astype(jnp.float32))
    pre = jnp.dot(normed_x.astype(jnp.bfloat16), full_in, preferred_element_type=jnp.float32)
    acts = jax.nn.silu(pre).astype(jnp.bfloat16)
    update_gate = acts[:, :width].astype(jnp.float32)
    values = acts[:, width : 2 * width]
    queries = acts[:, 2 * width : 3 * width]
    key_rows = acts[:, 3 * width :]
    keys_all, values_all = (
        lax.all_gather(key_rows, "ctx", axis=0, tiled=True),
        lax.all_gather(values, "ctx", axis=0, tiled=True),
    )
    query_heads = queries.reshape(rows, heads, head_size)

    def key_slices(start):
        key_block = lax.dynamic_slice_in_dim(keys_all, start, block, 0).reshape(
            block, heads, head_size
        )
        value_block = lax.dynamic_slice_in_dim(values_all, start, block, 0).reshape(
            block, heads, head_size
        )
        return (key_block, value_block)

    def forward_step(index, total):
        start = index * block
        key_pos = start + jnp.arange(block, dtype=jnp.int32)
        allowed = mask_block(own_pos, key_pos, boundary)
        key_block, value_block = key_slices(start)
        bias_slice = lax.dynamic_slice_in_dim(own_bias, start, block, 2)
        scores = score_block(query_heads, key_block, bias_slice, scale)
        weights = jnp.where(allowed[None], jax.nn.silu(scores) / seq, 0.0).astype(jnp.bfloat16)
        return total + jnp.einsum(
            "hrk,khd->rhd", weights, value_block, preferred_element_type=jnp.float32
        )

    attended = lax.fori_loop(
        0, seq // block, forward_step, jnp.zeros((rows, heads, head_size), jnp.float32)
    ).reshape(rows, width)
    normed_o, inverse_o = normalize(attended)
    gated = (normed_o * update_gate).astype(jnp.bfloat16)
    outputs = (
        inputs.astype(jnp.float32) + jnp.dot(gated, full_out, preferred_element_type=jnp.float32)
    ).astype(jnp.bfloat16)
    weight_term = lax.dot_general(
        gated, cotangent, (((0,), (0,)), ((), ())), preferred_element_type=jnp.float32
    )
    partial_rows = lax.psum_scatter(
        weight_term.astype(jnp.bfloat16), "dp", scatter_dimension=0, tiled=True
    )
    weight_grads = lax.psum_scatter(partial_rows, "ctx", scatter_dimension=1, tiled=True).astype(
        jnp.float32
    )
    d_gated = lax.dot_general(
        cotangent, full_out, (((1,), (1,)), ((), ())), preferred_element_type=jnp.float32
    )
    d_update = d_gated * normed_o
    d_attended = normalize_back(normed_o, inverse_o, d_gated * update_gate).astype(jnp.bfloat16)
    grad_heads = d_attended.reshape(rows, heads, head_size)

    def backward_step(index, carry):
        start = index * block
        key_pos = start + jnp.arange(block, dtype=jnp.int32)
        allowed = mask_block(own_pos, key_pos, boundary)
        d_queries, key_grads, value_grads = carry
        key_block, value_block = key_slices(start)
        bias_slice = lax.dynamic_slice_in_dim(own_bias, start, block, 2)
        weights, d_scores = attention_pair(
            query_heads, key_block, value_block, grad_heads, bias_slice, scale, seq, allowed
        )
        d_queries = d_queries + jnp.einsum(
            "hrk,khd->rhd", d_scores, key_block, preferred_element_type=jnp.float32
        )
        key_part = (
            jnp.einsum("hrk,rhd->khd", d_scores, query_heads, preferred_element_type=jnp.float32)
            * scale
        )
        value_part = jnp.einsum(
            "hrk,rhd->khd", weights, grad_heads, preferred_element_type=jnp.float32
        )
        key_grads = lax.dynamic_update_slice_in_dim(key_grads, key_part, start, 0)
        value_grads = lax.dynamic_update_slice_in_dim(value_grads, value_part, start, 0)
        return (d_queries, key_grads, value_grads)

    start_carry = (
        jnp.zeros((rows, heads, head_size), jnp.float32),
        jnp.zeros((seq, heads, head_size), jnp.float32),
        jnp.zeros((seq, heads, head_size), jnp.float32),
    )
    d_queries, key_grads, value_grads = lax.fori_loop(0, seq // block, backward_step, start_carry)
    key_sum, value_sum = (
        lax.psum_scatter(
            key_grads.reshape(seq, width).astype(jnp.bfloat16),
            "ctx",
            scatter_dimension=0,
            tiled=True,
        ).astype(jnp.float32),
        lax.psum_scatter(
            value_grads.reshape(seq, width).astype(jnp.bfloat16),
            "ctx",
            scatter_dimension=0,
            tiled=True,
        ).astype(jnp.float32),
    )
    d_acts = jnp.concatenate(
        [d_update, value_sum, (d_queries * scale).reshape(rows, width), key_sum], axis=1
    )
    d_pre = (d_acts * silu_grad(pre)).astype(jnp.bfloat16)
    d_normed = lax.dot_general(
        d_pre, full_in, (((1,), (1,)), ((), ())), preferred_element_type=jnp.float32
    )
    input_grads = (
        cotangent.astype(jnp.float32) + normalize_back(normed_x, inverse_x, d_normed)
    ).astype(jnp.bfloat16)
    return (outputs, input_grads, weight_grads)


def solution(mesh):
    return jax.shard_map(
        on_device,
        mesh=mesh,
        in_specs=(
            P(("dp", "ctx"), None),
            P("dp", None),
            P("dp", None),
            P(("dp", "ctx"), None),
            P("dp", None),
            P(),
            P(),
        ),
        out_specs=(P(("dp", "ctx"), None), P(("dp", "ctx"), None), P("dp", "ctx")),
        check_vma=False,
    )
```

profile of v0, /device:TPU:1, one launch (start us, length us, event | category | flops | bytes accessed | tf_op | source)
XLA Modules:
  0.0 1013.4 jit_solution(16834548972343670746)
XLA Ops:
  10.2 154.1 %all-gather.5.cloned.1.call-done = bf16[1024,4096]{1,0:T(8,128)(2,1)} async-done(((bf16[32,4096]{1,0:T(8,128)(2,1)}), bf16[1024,4096]{1,0:T(8,128)(2,1)}) %all-gather.5.cloned.1.call-update) | async-done | bytes 8388624 | tf_op jit(solution)/shard_map/all_gather | solution.py:67
  164.3 6.3 multiply_convert_fusion
  174.2 2.8 gather_fusion
  177.1 430.4 %gather_fusion.1 = f32[131072,8]{1,0:T(8,128)} fusion(f32[8,1024]{0,1:T(8,128)S(1)} %bitcast.136, s32[131072]{0:T(1024)S(1)} %broadcast_clamp_fusion), kind=kCustom, calls=%fused_computation.1 | custom fusion | bytes 8912896 | tf_op jit(solution)/shard_map/jit(_take)/gather | solution.py:74
  607.5 36.0 %copy.65 = f32[128,1024,8]{0,1,2:T(8,128)} copy(f32[128,1024,8]{2,1,0:T(8,128)} %bitcast.3) | data formatting | bytes 8388608 | tf_op jit(solution)/shard_map/jit(_take)/gather | solution.py:74
  643.8 4.5 select_bitcast_fusion
  648.4 4.0 copy.66
  652.3 4.0 copy.67
  656.3 10.1 while.32
  656.7 1.7 constant_dynamic-slice_fusion.6
  658.4 2.9 fusion.93
  661.7 1.7 constant_dynamic-slice_fusion.6
  663.4 2.9 fusion.93
  667.7 2.5 fusion.48
  671.5 1.6 broadcast.310
  673.1 1.6 broadcast.310.clone
  674.7 17.1 %while.33 = (s32[]{:T(128)}, f32[128,8,128]{0,2,1:T(8,128)S(1)}, bf16[1024,8,128]{2,0,1:T(8,128)(2,1)}, bf16[1024,8,128]{2,0,1:T(8,128)(2,1)}, bf16[1024,1024]{0...) while((s32[]{:T(128)}, f32[128,8,128]{0,2,1:T(8,128)S(1)}, ...), condition=%wide.region_14.15_spmd.clone, body=%wide.region_11.14_spmd.clone.sunk | while | flops 682565120 | bytes 42152728 | solution.py:162
  674.7 1.8 constant_dynamic-slice_fusion.7
  681.0 1.7 bitcast_dynamic-update-slice_fusion.5
  683.2 1.8 constant_dynamic-slice_fusion.7
  688.2 1.4 bitcast_dynamic-update-slice_fusion.4
  689.6 1.7 bitcast_dynamic-update-slice_fusion.5
  691.8 3.2 copy_bitcast_fusion.1
  695.1 3.3 copy_bitcast_fusion
  699.3 2.1 convolution_convert_fusion
  702.5 2.0 copy.83
  705.7 51.5 %reduce-scatter.7.cloned.1.call-done = bf16[128,1024]{1,0:T(8,128)(2,1)} async-done(((bf16[1024,1024]{1,0:T(8,128)(2,1)}), bf16[128,1024]{1,0:T(8,128)(2,1)}) %reduce-scatter.7.cloned.1.call-update) | async-done | bytes 262160 | tf_op jit(solution)/shard_map/reduce_scatter | solution.py:170
  758.2 43.8 %reduce-scatter.9.cloned.1.call-done = bf16[128,1024]{1,0:T(8,128)(2,1)} async-done(((bf16[1024,1024]{1,0:T(8,128)(2,1)}), bf16[128,1024]{1,0:T(8,128)(2,1)}) %reduce-scatter.9.cloned.1.call-update) | async-done | bytes 262160 | tf_op jit(solution)/shard_map/reduce_scatter | solution.py:164
  803.0 7.4 fusion.52
  810.4 135.9 %reduce-scatter.11.cloned.1.call-done = bf16[32,1024]{1,0:T(8,128)(2,1)} async-done(((bf16[1024,1024]{1,0:T(8,128)(2,1)}), bf16[32,1024]{1,0:T(8,128)(2,1)}) %reduce-scatter.11.cloned.1.call-update) | async-done | bytes 65552 | tf_op jit(solution)/shard_map/reduce_scatter | solution.py:120
  946.3 1.7 copy.84
  949.0 56.1 %reduce-scatter.13.cloned.1.call-done = bf16[128,32]{1,0:T(8,128)(2,1)} async-done(((bf16[1024,32]{1,0:T(8,128)(2,1)}), bf16[128,32]{1,0:T(8,128)(2,1)}) %reduce-scatter.13.cloned.1.call-update) | async-done | bytes 8208
  (101 shorter events, 26.4 us)
Async XLA Ops:
  7.2 157.1 %all-gather.5.cloned.1.call-start = ((), (), s32[]{:S(2)}) async-start(), calls=%async_computation.4 | async-start | bytes 8650752 | tf_op jit(solution)/shard_map/all_gather | solution.py:67
  7.9 640.5 %all-gather.7.cloned.1.call-start = ((), (), s32[]{:S(2)}) async-start(), calls=%async_computation.5 | async-start | bytes 2359296 | tf_op jit(solution)/shard_map/all_gather | solution.py:84
  170.6 1.0 copy-start.5
  171.5 2.6 copy-start.7
  171.6 2.7 copy-start.8
  172.4 479.9 %all-gather.9.cloned.1.call-start = ((), (), s32[]{:S(2)}) async-start(), calls=%async_computation.6 | async-start | bytes 2359296 | tf_op jit(solution)/shard_map/all_gather | solution.py:83
  173.2 493.8 %all-gather.11.cloned.1.call-start = ((), (), s32[]{:S(2)}) async-start(), calls=%async_computation.7 | async-start | bytes 2162688 | tf_op jit(solution)/shard_map/all_gather | solution.py:68
  173.8 583.4 %reduce-scatter.7.cloned.1.call-start = ((), (), s32[]{:S(2)}) async-start(), calls=%async_computation.8 | async-start | bytes 2359296 | tf_op jit(solution)/shard_map/reduce_scatter | solution.py:170
  607.5 36.0 %copy-start.9 = (s32[1,4]{1,0:T(1,128)S(1)}, s32[1,4]{1,0:T(1,128)}, u32[]{:S(2)}) copy-start(s32[1,4]{1,0:T(1,128)} %param.15) | copy-start | bytes 52
  666.4 1.0 copy-start.3
  666.4 1.3 copy-start.6
  674.7 2.8 copy-start
  683.2 2.8 copy-start
  695.0 107.0 %reduce-scatter.9.cloned.1.call-start = ((), (), s32[]{:S(2)}) async-start(), calls=%async_computation.9 | async-start | bytes 2359296 | tf_op jit(solution)/shard_map/reduce_scatter | solution.py:164
  698.3 0.9 copy-start.4
  698.4 247.9 %reduce-scatter.11.cloned.1.call-start = ((), (), s32[]{:S(2)}) async-start(), calls=%async_computation.10 | async-start | bytes 2162688 | tf_op jit(solution)/shard_map/reduce_scatter | solution.py:120
  701.4 3.2 copy-start.1
  701.4 3.2 copy-start.2
  701.4 303.7 %reduce-scatter.13.cloned.1.call-start = ((), (), s32[]{:S(2)}) async-start(), calls=%async_computation.11 | async-start | bytes 294912
Sparse Core Ops, SparseCore 0:
  9.8 154.4 all-gather.4
  172.6 57.1 all-gather.6
  232.2 34.0 all-gather.8
  268.0 132.3 all-gather.10
  695.2 61.9 reduce-scatter.6
  759.6 42.3 reduce-scatter.8
  804.5 141.7 reduce-scatter.10
  949.0 56.0 reduce-scatter.12
where the time goes:
time: 1020 us; the launch traced here: 1010 us
  local copies, waits for them, and re-layouts  504 us (49%)
  waiting for transfers between devices  443 us (43%)
  matrix products  35.9 us (4%)
  other arithmetic  14.7 us (1%)
  between operations  14.3 us (1%)
    gather x2, local copies, waits for them, and re-layouts, on_device(): jnp.take(bias_table, jnp.maximum(own_pos[:, None] - all_pos[None, :], 0),...  466 us
    all_gather x1, waiting for transfers between devices, on_device(): lax.all_gather(input_weight, 'dp', axis=0, tiled=True)  154 us
    reduce_scatter x1, waiting for transfers between devices, on_device(): lax.psum_scatter(weight_term.astype(jnp.bfloat16), 'dp', scatter_dimensio...  136 us
    unnamed x9, waiting for transfers between devices  58.1 us
    reduce_scatter x1, waiting for transfers between devices, on_device(): lax.psum_scatter(value_grads.reshape(seq, width).astype(jnp.bfloat16), 'c...  51.5 us
    reduce_scatter x1, waiting for transfers between devices, on_device(): lax.psum_scatter(key_grads.reshape(seq, width).astype(jnp.bfloat16), 'ctx...  43.8 us
  transfers between devices with their start and end apart: 8, of which 5 were waited for; matrix products, arithmetic and copies ran while one was open for 51% of the time, Pallas kernels for 0%

commit v1 on v0

v1 whole, which is shorter than its diff:
```python
import functools
import math

import jax
import jax.numpy as jnp
from jax import lax
from jax.experimental import pallas as pl
from jax.experimental.pallas import tpu as pltpu
from jax.sharding import PartitionSpec as P

EPSILON = 1e-06
MESH = pl.DeviceIdType.MESH
F32 = jnp.float32
BF16 = jnp.bfloat16

ROWS = 128
BLK = 256
NBLK = 4
HEADS = 8
HD = 128
D = 1024
SEQ = 1024
PLANE = 16
PAIRS = NBLK * (NBLK + 1) // 2
SCALE = 1.0 / math.sqrt(HD)


def nn(a, b):
    return lax.dot_general(a, b, (((1,), (0,)), ((), ())), preferred_element_type=F32)


def nt(a, b):
    return lax.dot_general(a, b, (((1,), (1,)), ((), ())), preferred_element_type=F32)


def tn(a, b):
    return lax.dot_general(a, b, (((0,), (0,)), ((), ())), preferred_element_type=F32)


def sigmoid(values):
    return 0.5 * jnp.tanh(0.5 * values) + 0.5


def normalize(values):
    average = jnp.mean(values, axis=-1, keepdims=True)
    centered = values - average
    inverse = lax.rsqrt(jnp.mean(centered * centered, axis=-1, keepdims=True) + EPSILON)
    return (centered * inverse, inverse)


def kernel(
    lengths_ref, bias_ref, buckets_ref, x_ref, win_ref, wout_ref, ct_ref,
    out_ref, grads_ref, wg_ref,
    xg, wa, wb, wra, wrb, wct, pret, actt, krow, vrow, wts, sgs, toep, attt, uf,
    dgs, dgr, stat, statr, gts, gtr, dat, dqt, dkt, dvt, dpt,
    wgd, wgdr, wgs, wgr, wzs, wzr,
    pd, pdr, ps, pr, own,
    xs, xr, xfs, xfr, was, war, wps, wpr, wos, wor, dss, dsr, sts, strr, gss, gsr,
    wds, wdr, wgss, wgsr, wzss, wzsr, pds, pdsr, pss, psr,
):
    dp = lax.axis_index("dp")
    ctx = lax.axis_index("ctx")
    zh, core = ctx // 2, ctx % 2
    zl, yx = dp // PLANE, dp % PLANE
    y, x = yx // 4, yx % 4
    mate = (dp, zh * 2 + 1 - core)

    def ctx_peer(t):
        return (ctx + t) % 8

    def plane_peer(t):
        return ((y + t // 4) % 4) * 4 + (x + t % 4) % 4

    def plane_from(t):
        return ((y + 4 - t // 4) % 4) * 4 + (x + 4 - t % 4) % 4

    def copy(src, dst, ss, rs, dev):
        return pltpu.make_async_remote_copy(
            src_ref=src, dst_ref=dst, send_sem=ss, recv_sem=rs, device_id=dev, device_id_type=MESH
        )

    barrier = pltpu.get_barrier_semaphore()

    def greet_ctx(t, _):
        pl.semaphore_signal(barrier, inc=1, device_id=(dp, ctx_peer(t)), device_id_type=MESH)
        return 0

    def greet_plane(t, _):
        pl.semaphore_signal(
            barrier, inc=1, device_id=(zl * PLANE + plane_peer(t), ctx), device_id_type=MESH
        )
        return 0

    def greet_column(t, _):
        pl.semaphore_signal(
            barrier, inc=1, device_id=((1 - zl) * PLANE + yx, t * 2 + core), device_id_type=MESH
        )
        return 0

    lax.fori_loop(1, 8, greet_ctx, 0)
    lax.fori_loop(1, 16, greet_plane, 0)
    lax.fori_loop(0, 4, greet_column, 0)

    normed, _ = normalize(x_ref[...].astype(F32))
    xg[ctx] = normed.astype(BF16)
    for part in range(4):
        at = pl.multiple_of(part * D + ctx * HD, HD)
        wa[zl, :, part * HD:(part + 1) * HD] = win_ref[:, pl.ds(at, HD)]
    wb[zl] = wout_ref[:, pl.ds(pl.multiple_of(core * 512, 512), 512)]

    pl.semaphore_wait(barrier, 26)

    other = ((1 - zl) * PLANE + yx, ctx)
    send_wa = copy(wa.at[zl], wa.at[zl], was.at[0], war.at[0], other)
    send_wa.start()
    send_x = [copy(xg.at[ctx], xg.at[ctx], xs.at[0], xr.at[0], mate)]
    for s in (2, 1, 3):
        send_x.append(
            copy(xg.at[ctx], xg.at[ctx], xs.at[s], xr.at[s], (dp, ((zh + s) % 4) * 2 + core))
        )
    for c in send_x:
        c.start()
    send_wb = copy(wb.at[zl], wb.at[zl], was.at[1], war.at[1], other)
    send_wb.start()

    def plane_send(src, dst, base):
        def step(t, _):
            copy(
                src, dst.at[:, yx], wps.at[base + t], wpr.at[base + t],
                (zl * PLANE + plane_peer(t), ctx),
            ).start()
            return 0
        lax.fori_loop(1, 16, step, 0)

    def plane_recv(src, dst, base):
        def step(t, _):
            copy(
                src, dst.at[:, plane_from(t)], wps.at[base + t], wpr.at[base + t],
                (zl * PLANE + plane_peer(t), ctx),
            ).wait_recv()
            return 0
        lax.fori_loop(1, 16, step, 0)

    def plane_done(src, dst, base):
        def step(t, _):
            copy(
                src, dst.at[:, yx], wps.at[base + t], wpr.at[base + t],
                (zl * PLANE + plane_peer(t), ctx),
            ).wait_send()
            return 0
        lax.fori_loop(1, 16, step, 0)

    send_wa.wait_recv()
    plane_send(wa, wra, 0)
    wra[:, yx] = wa[...]

    buckets = buckets_ref[...]
    table = jnp.zeros((1, SEQ), F32)
    for b in range(32):
        table = jnp.where(buckets == b, bias_ref[ctx, b], table)
    padded = jnp.concatenate([table[:, 0:BLK], table], axis=1)
    for d in range(NBLK):
        wide = jnp.broadcast_to(padded[:, d * BLK:d * BLK + 2 * BLK], (BLK, 2 * BLK))
        toep[d] = pltpu.roll(wide, 0, 1, stride=1, stride_axis=0)[:, BLK:]

    send_wb.wait_recv()
    wrb[core, :, yx] = wb[...]
    plane_recv(wa, wra, 0)
    plane_send(wb, wrb.at[core], 16)

    for part in range(4):
        piece = wra[:, :, :, part * HD:(part + 1) * HD].reshape(D, HD)
        wct[part * HD:(part + 1) * HD, :] = piece.T

    def project(zb):
        rows = xg[pl.ds(zb * 2, 2)].reshape(BLK, D)
        pre = nt(wct[...], rows)
        pret[zb] = pre
        acts = (pre * sigmoid(pre)).astype(BF16)
        actt[zb] = acts
        vrow[zb] = acts[HD:2 * HD].T
        krow[zb] = acts[3 * HD:].T

    def forward_x(s):
        src = ((zh + 4 - s) % 4) * 2 + core
        return copy(xg.at[src], xg.at[src], xfs.at[s], xfr.at[s], mate)

    def arrived_x(s):
        src = ((zh + 4 - s) % 4) * 2 + core
        copy(xg.at[ctx], xg.at[src], xs.at[s], xr.at[s], (dp, ((zh + s) % 4) * 2 + core)).wait_recv()

    send_x[0].wait_recv()
    project(zh)
    for s in (1, 3):
        arrived_x(s)
        forward_x(s).start()
    for s in (1, 3):
        forward_x(s).wait_recv()
        project((zh + 4 - s) % 4)
    arrived_x(2)
    forward_x(2).start()
    forward_x(2).wait_recv()
    project((zh + 2) % 4)

    plane_recv(wb, wrb.at[core], 16)
    send_wo = copy(wrb.at[core], wrb.at[core], wos.at[0], wor.at[0], mate)
    send_wo.start()
    ctv = ct_ref[...]

    l0, l1, l2 = lengths_ref[0, 0], lengths_ref[0, 1], lengths_ref[0, 2]
    e0, e1, e2 = l0, l0 + l1, l0 + l1 + l2

    def pair_of(p):
        i = (p >= 1).astype(jnp.int32) + (p >= 3).astype(jnp.int32) + (p >= 6).astype(jnp.int32)
        return i, p - (i * (i + 1)) // 2

    attt[...] = jnp.zeros_like(attt)

    def forward(p, _):
        i, j = pair_of(p)
        scores = nn(krow[j], actt[i, 2 * HD:3 * HD, :]) * SCALE + toep[i - j]
        qpos = i * BLK + lax.broadcasted_iota(jnp.int32, (1, BLK), 1)
        first = jnp.where(qpos >= e2, e2, jnp.where(qpos >= e1, e1, jnp.where(qpos >= e0, e0, 0)))
        kpos = j * BLK + lax.broadcasted_iota(jnp.int32, (BLK, BLK), 0)
        allowed = (kpos >= first) & (kpos <= qpos)
        sig = sigmoid(scores)
        act = scores * sig
        weights = jnp.where(allowed, act * (1.0 / SEQ), 0.0).astype(BF16)
        wts[p] = weights
        sgs[p] = jnp.where(allowed, (sig + act * (1.0 - sig)) * (1.0 / SEQ), 0.0)
        attt[i] += nn(actt[j, HD:2 * HD, :], weights)
        return 0

    lax.fori_loop(0, PAIRS, forward, 0)

    send_wo.wait_recv()
    dgt = (
        nt(wrb[0].reshape(D, 512), ctv[:, 0:512]) + nt(wrb[1].reshape(D, 512), ctv[:, 512:])
    ).astype(BF16)
    for h in range(HEADS):
        dgs[h] = dgt[h * HD:(h + 1) * HD]

    def ctx_copy(t, src, dst, ss, rs):
        return copy(src, dst, ss.at[t], rs.at[t], (dp, ctx_peer(t)))

    def each(lo, hi, body):
        def step(t, _):
            body(t)
            return 0
        lax.fori_loop(lo, hi, step, 0)

    def from_ctx(t):
        return (ctx + 8 - t) % 8

    each(1, 8, lambda t: ctx_copy(t, dgs.at[ctx_peer(t)], dgr.at[ctx], dss, dsr).start())
    dgr[ctx] = dgs[ctx]
    each(1, 8, lambda t: ctx_copy(t, dgs.at[ctx_peer(t)], dgr.at[from_ctx(t)], dss, dsr).wait_recv())

    def dg_block(b):
        return jnp.concatenate([dgr[2 * b], dgr[2 * b + 1]], axis=1).astype(F32)

    for b in range(NBLK):
        att = attt[b]
        up = dg_block(b) * actt[b, 0:HD, :].astype(F32)
        mean = jnp.sum(att, axis=0, keepdims=True) * (1.0 / HD)
        cen = att - mean
        rows = [
            mean,
            jnp.sum(cen * cen, axis=0, keepdims=True),
            jnp.sum(up, axis=0, keepdims=True),
            jnp.sum(up * cen, axis=0, keepdims=True),
        ]
        stat[b] = jnp.concatenate(rows + [jnp.zeros((4, BLK), F32)], axis=0)
    statr[ctx] = stat[...]
    each(1, 8, lambda t: ctx_copy(t, stat, statr.at[ctx], sts, strr).start())
    each(1, 8, lambda t: ctx_copy(t, stat, statr.at[from_ctx(t)], sts, strr).wait_recv())

    dqt[...] = jnp.zeros_like(dqt)
    dkt[...] = jnp.zeros_like(dkt)
    dvt[...] = jnp.zeros_like(dvt)
    for b in range(NBLK):
        parts = [statr[r, b] for r in range(HEADS)]
        mean = sum([q[0:1] for q in parts]) * (1.0 / HEADS)
        var, s3, s4 = 0.0, 0.0, 0.0
        for q in parts:
            off = q[0:1] - mean
            var = var + q[1:2] + HD * off * off
            s3 = s3 + q[2:3]
            s4 = s4 + q[3:4] + off * q[2:3]
        inv = lax.rsqrt(var * (1.0 / D) + EPSILON)
        m1 = s3 * (1.0 / D)
        m2 = s4 * inv * (1.0 / D)
        norm = (attt[b] - mean) * inv
        dg = dg_block(b)
        u = actt[b, 0:HD, :].astype(F32)
        gated = (norm * u).astype(BF16)
        gts[2 * b] = gated[:, 0:ROWS]
        gts[2 * b + 1] = gated[:, ROWS:]
        dat[b] = ((dg * u - m1 - norm * m2) * inv).astype(BF16)
        uf[b] = dg * norm

    each(1, 8, lambda t: ctx_copy(t, gts.at[ctx_peer(t)], gtr.at[ctx], gss, gsr).start())
    gtr[ctx] = gts[ctx]

    def backward(p, _):
        i, j = pair_of(p)
        da = dat[i]
        ds = (nn(vrow[j], da) * sgs[p]).astype(BF16)
        dqt[i] += nn(actt[j, 3 * HD:, :], ds)
        dkt[j] += nt(actt[i, 2 * HD:3 * HD, :], ds)
        dvt[j] += nt(da, wts[p])
        return 0

    lax.fori_loop(0, PAIRS, backward, 0)

    for b in range(NBLK):
        for part, val in enumerate((uf[b], dvt[b], dqt[b] * SCALE, dkt[b] * SCALE)):
            pre = pret[b, part * HD:(part + 1) * HD, :]
            sig = sigmoid(pre)
            dpt[b, part * HD:(part + 1) * HD, :] = (
                val * (sig * (1.0 + pre * (1.0 - sig)))
            ).astype(BF16)

    def mate_copy(b):
        return copy(pd.at[b], pdr.at[b], pds.at[b], pdsr.at[b], mate)

    for s in (2, 1, 3, 0):
        b = (zh + s) % 4
        col = pl.multiple_of((1 - core) * ROWS, ROWS)
        pd[b] = tn(dpt[b, :, pl.ds(col, ROWS)], wct[...]).astype(BF16)
        mate_copy(b).start()

    def row_copy(s):
        return copy(ps.at[s], pr.at[s], pss.at[s], psr.at[s], (dp, ((zh + s) % 4) * 2 + core))

    for s in (2, 1, 3, 0):
        b = (zh + s) % 4
        col = pl.multiple_of(core * ROWS, ROWS)
        mine = tn(dpt[b, :, pl.ds(col, ROWS)], wct[...])
        mate_copy(b).wait_recv()
        both = mine + pdr[b].astype(F32)
        if s:
            ps[s] = both.astype(BF16)
            row_copy(s).start()
        else:
            own[...] = both

    each(1, 8, lambda t: ctx_copy(t, gts.at[ctx_peer(t)], gtr.at[from_ctx(t)], gss, gsr).wait_recv())
    gt = gtr[...].reshape(D, ROWS)
    for half in range(2):
        cols = slice(half * 512, half * 512 + 512)
        out_ref[:, cols] = (
            x_ref[:, cols].astype(F32) + tn(gt, wrb[half].reshape(D, 512))
        ).astype(BF16)

    def ct_cols(which):
        return jnp.concatenate(
            [ct_ref[:, pl.ds(pl.multiple_of(b * BLK + which * HD, HD), HD)] for b in range(NBLK)], axis=1
        )

    wgd[...] = nn(gt, ct_cols(1 - core)).astype(BF16)
    send_wg = copy(wgd, wgdr, wds.at[0], wdr.at[0], mate)
    send_wg.start()
    wmine = nn(gt, ct_cols(core))
    send_wg.wait_recv()
    wgs[...] = (wmine + wgdr[...].astype(F32)).astype(BF16).reshape(2, PLANE, 32, 512)

    def wg_copy(t, to):
        return copy(
            wgs.at[:, plane_peer(t)], wgr.at[to], wgss.at[t], wgsr.at[t],
            (zl * PLANE + plane_peer(t), ctx),
        )

    each(1, 16, lambda t: wg_copy(t, yx).start())
    wgr[yx] = wgs[:, yx]
    each(1, 16, lambda t: wg_copy(t, plane_from(t)).wait_recv())

    def add_plane(t, total):
        return total + wgr[t].astype(F32)

    wsum = lax.fori_loop(0, PLANE, add_plane, jnp.zeros((2, 32, 512), F32)).astype(BF16)
    for l in range(2):
        for h in range(4):
            wzs[l * 4 + h] = wsum[l, :, h * HD:(h + 1) * HD]

    zat = zl * 4 + zh

    def wz_copy(t, slot):
        to = (zat + t) % 8
        return copy(
            wzs.at[to], wzr.at[slot], wzss.at[t], wzsr.at[t],
            ((to // 4) * PLANE + yx, (to % 4) * 2 + core),
        )

    each(1, 8, lambda t: wz_copy(t, zat).start())
    wzr[zat] = wzs[zat]

    total = own[...]
    for s in (1, 3, 2):
        row_copy(s).wait_recv()
        total = total + pr[s].astype(F32)
    normed, inverse = normalize(x_ref[...].astype(F32))
    first = jnp.mean(total, axis=-1, keepdims=True)
    second = jnp.mean(total * normed, axis=-1, keepdims=True)
    grads_ref[...] = (
        ct_ref[...].astype(F32) + (total - first - normed * second) * inverse
    ).astype(BF16)

    each(1, 8, lambda t: wz_copy(t, (zat + 8 - t) % 8).wait_recv())
    wg_ref[...] = jnp.sum(wzr[...].astype(F32), axis=0)

    send_wa.wait_send()
    send_wb.wait_send()
    for c in send_x:
        c.wait_send()
    for s in (1, 2, 3):
        forward_x(s).wait_send()
        row_copy(s).wait_send()
    plane_done(wa, wra, 0)
    plane_done(wb, wrb.at[core], 16)
    send_wo.wait_send()
    send_wg.wait_send()
    each(1, 8, lambda t: ctx_copy(t, dgs.at[ctx_peer(t)], dgr.at[ctx], dss, dsr).wait_send())
    each(1, 8, lambda t: ctx_copy(t, stat, statr.at[ctx], sts, strr).wait_send())
    each(1, 8, lambda t: ctx_copy(t, gts.at[ctx_peer(t)], gtr.at[ctx], gss, gsr).wait_send())
    for b in range(NBLK):
        mate_copy(b).wait_send()
    each(1, 16, lambda t: wg_copy(t, yx).wait_send())
    each(1, 8, lambda t: wz_copy(t, zat).wait_send())


def on_device(inputs, input_weight, output_weight, cotangent, lengths, buckets, bias_weights):
    vm = lambda *shape, dt=BF16: pltpu.VMEM(shape, dt)
    sem = lambda n: pltpu.SemaphoreType.DMA((n,))
    scratch = [
        vm(8, ROWS, D), vm(2, 32, 512), vm(2, 32, 512),
        vm(2, PLANE, 32, 512), vm(2, 2, PLANE, 32, 512),
        vm(512, D), vm(NBLK, 512, BLK, dt=F32), vm(NBLK, 512, BLK),
        vm(NBLK, BLK, HD), vm(NBLK, BLK, HD),
        vm(PAIRS, BLK, BLK), vm(PAIRS, BLK, BLK, dt=F32), vm(NBLK, BLK, BLK, dt=F32),
        vm(NBLK, HD, BLK, dt=F32), vm(NBLK, HD, BLK, dt=F32),
        vm(8, HD, ROWS), vm(8, HD, ROWS),
        vm(NBLK, 8, BLK, dt=F32), vm(8, NBLK, 8, BLK, dt=F32),
        vm(8, HD, ROWS), vm(8, HD, ROWS), vm(NBLK, HD, BLK),
        vm(NBLK, HD, BLK, dt=F32), vm(NBLK, HD, BLK, dt=F32), vm(NBLK, HD, BLK, dt=F32),
        vm(NBLK, 512, BLK),
        vm(D, 512), vm(D, 512), vm(2, PLANE, 32, 512), vm(PLANE, 2, 32, 512),
        vm(8, 32, HD), vm(8, 32, HD),
        vm(NBLK, ROWS, D), vm(NBLK, ROWS, D), vm(4, ROWS, D), vm(4, ROWS, D), vm(ROWS, D, dt=F32),
        sem(4), sem(4), sem(4), sem(4), sem(2), sem(2), sem(32), sem(32), sem(1), sem(1),
        sem(8), sem(8), sem(8), sem(8), sem(8), sem(8),
        sem(1), sem(1), sem(16), sem(16), sem(8), sem(8), sem(4), sem(4), sem(4), sem(4),
    ]
    vspec = pl.BlockSpec(memory_space=pltpu.VMEM)
    sspec = pl.BlockSpec(memory_space=pltpu.SMEM)
    return pl.pallas_call(
        kernel,
        name="hstu",
        out_shape=(
            jax.ShapeDtypeStruct((ROWS, D), BF16),
            jax.ShapeDtypeStruct((ROWS, D), BF16),
            jax.ShapeDtypeStruct((32, HD), F32),
        ),
        in_specs=[sspec, sspec, vspec, vspec, vspec, vspec, vspec],
        out_specs=(vspec, vspec, vspec),
        scratch_shapes=scratch,
        compiler_params=pltpu.CompilerParams(
            collective_id=0, has_side_effects=True, vmem_limit_bytes=56 << 20
        ),
    )(lengths, bias_weights, buckets.reshape(1, SEQ), inputs, input_weight, output_weight, cotangent)


def solution(mesh):
    return jax.shard_map(
        on_device,
        mesh=mesh,
        in_specs=(
            P(("dp", "ctx"), None),
            P("dp", None),
            P("dp", None),
            P(("dp", "ctx"), None),
            P("dp", None),
            P(),
            P(),
        ),
        out_specs=(P(("dp", "ctx"), None), P(("dp", "ctx"), None), P("dp", "ctx")),
        check_vma=False,
    )
```

time: 1020 us -> 116 us (0.11)
  local copies, waits for them, and re-layouts: 504 us -> 3.04 us
  waiting for transfers between devices: 443 us -> 0 us
  Pallas kernels: 0 us -> 112 us
  matrix products: 35.9 us -> 0 us
  other arithmetic: 14.7 us -> 0 us
  between operations: 14.3 us -> 0.65 us
    gather x3 -> x0, local copies, waits for them, and re-layouts: 469 us -> none  [the longest x2 466 us: on_device(): jnp.take(bias_table, jnp.maximum(own_pos[:, None] - all_pos[None, :], 0),...]
    reduce_scatter x3 -> x0, waiting for transfers between devices: 231 us -> none  [the longest x1 136 us: on_device(): lax.psum_scatter(weight_term.astype(jnp.bfloat16), 'dp', scatter_dimensio...]
    all_gather x4 -> x0, waiting for transfers between devices: 154 us -> none  [the longest x1 154 us: on_device(): lax.all_gather(input_weight, 'dp', axis=0, tiled=True)]
    pallas_call x0 -> x1, Pallas kernels: none -> 112 us  [on_device(): pl.pallas_call(kernel, name='hstu', out_shape=(jax.ShapeDtypeStruct((ROWS...]
    unnamed x9 -> x0, waiting for transfers between devices: 58.1 us -> none
    dot_general x17 -> x0, matrix products: 35.9 us -> none  [the longest x1 7.38 us: on_device(): lax.dot_general(d_pre, full_in, (((1,), (1,)), ((), ())), preferred_eleme...]
    unnamed x25 -> x7, local copies, waits for them, and re-layouts: 14.1 us -> 3.04 us
  transfers between devices with their start and end apart: 8 -> 0, of which waited for: 5 -> 0; matrix products, arithmetic and copies ran while one was open for 51% -> 0% of each run, Pallas kernels for 0% -> 0%
where the time goes in v1:
time: 116 us
  Pallas kernels  112 us (97%)
  local copies, waits for them, and re-layouts  3.04 us (3%)
    pallas_call x1, Pallas kernels, on_device(): pl.pallas_call(kernel, name='hstu', out_shape=(jax.ShapeDtypeStruct((ROWS...  112 us
    unnamed x7, local copies, waits for them, and re-layouts  3.04 us

profile of v1, /device:TPU:1, one launch (start us, length us, event | category | flops | bytes accessed | tf_op | source)
XLA Modules:
  0.0 115.9 jit_solution(15583775290431068333)
XLA Ops:
  0.6 112.2 %hstu.1 = (bf16[128,1024]{1,0:T(8,128)(2,1)}, bf16[128,1024]{1,0:T(8,128)(2,1)}, f32[32,128]{1,0:T(8,128)}) custom-call(s32[1,4]{1,0:T(1,128)} %lengths_ref.1, f32[8,32]{1,0:T(8,128)} %bias_ref.1, s32[1,1024]{1,0:T(1,128)} %bitcast.1, bf16[128,1024]{1,0:T(8,128)(2,1)} %x_ref.1, bf16[32,4096]{1,0:T(8,128)(2,1)} %win_ref.1, bf16[32,1024]{1,0:T(8,128)(2,1)} %wout_ref.1, ...), custom_call_target="tpu_custom_call" | custom-call | tf_op jit(solution)/shard_map/hstu/pallas_call | solution.py:456
  112.8 0.0 copy-start
  112.8 1.7 %copy.13 = bf16[128,1024]{1,0:T(8,128)(2,1)} copy(bf16[128,1024]{1,0:T(8,128)(2,1)} %get-tuple-element.6) | data formatting | bytes 524288
  114.5 0.0 copy-done
  114.5 0.0 copy-start.1
  114.5 0.7 copy.14
  115.2 0.0 copy-done.1
  115.3 0.6 copy.15
Async XLA Ops:
  112.8 1.7 %copy-start = (bf16[128,1024]{1,0:T(8,128)(2,1)S(1)}, bf16[128,1024]{1,0:T(8,128)(2,1)}, u32[]{:S(2)}) copy-start(bf16[128,1024]{1,0:T(8,128)(2,1)} %get-tuple-element.7) | copy-start | bytes 786436
  114.5 0.7 copy-start.1

commit v2 on v1

v2 whole, which is shorter than its diff:
```python
import functools
import math

import jax
import jax.numpy as jnp
from jax import lax
from jax.experimental import pallas as pl
from jax.experimental.pallas import tpu as pltpu
from jax.sharding import PartitionSpec as P

EPSILON = 1e-06
MESH = pl.DeviceIdType.MESH
F32 = jnp.float32
BF16 = jnp.bfloat16

ROWS = 128
BLK = 256
NBLK = 4
HEADS = 8
HD = 128
D = 1024
SEQ = 1024
PLANE = 16
PAIRS = NBLK * (NBLK + 1) // 2
SCALE = 1.0 / math.sqrt(HD)


def nn(a, b):
    return lax.dot_general(a, b, (((1,), (0,)), ((), ())), preferred_element_type=F32)


def nt(a, b):
    return lax.dot_general(a, b, (((1,), (1,)), ((), ())), preferred_element_type=F32)


def tn(a, b):
    return lax.dot_general(a, b, (((0,), (0,)), ((), ())), preferred_element_type=F32)


def sigmoid(values):
    return 0.5 * jnp.tanh(0.5 * values) + 0.5


def normalize(values):
    average = jnp.mean(values, axis=-1, keepdims=True)
    centered = values - average
    inverse = lax.rsqrt(jnp.mean(centered * centered, axis=-1, keepdims=True) + EPSILON)
    return (centered * inverse, inverse)


def kernel(
    lengths_ref, bias_ref, buckets_ref, x_ref, win_ref, wout_ref, ct_ref,
    out_ref, grads_ref, wg_ref,
    xg, wa, wb, wra, wrb, wct, pret, actt, krow, vrow, wts, sgs, toep, attt, uf,
    dgs, dgr, stat, statr, gts, gtr, dat, dqt, dkt, dvt, dpt,
    wgd, wgdr, wgs, wgr, wzs, wzr,
    pd, pdr, ps, pr, own,
    xs, xr, xfs, xfr, was, war, wps, wpr, wos, wor, dss, dsr, sts, strr, gss, gsr,
    wds, wdr, wgss, wgsr, wzss, wzsr, pds, pdsr, pss, psr,
):
    dp = lax.axis_index("dp")
    ctx = lax.axis_index("ctx")
    zh, core = ctx // 2, ctx % 2
    zl, yx = dp // PLANE, dp % PLANE
    y, x = yx // 4, yx % 4
    mate = (dp, zh * 2 + 1 - core)

    def ctx_peer(t):
        return (ctx + t) % 8

    def plane_peer(t):
        return ((y + t // 4) % 4) * 4 + (x + t % 4) % 4

    def plane_from(t):
        return ((y + 4 - t // 4) % 4) * 4 + (x + 4 - t % 4) % 4

    started = []

    class Copies:
        def __init__(self, make, lo=0, hi=1):
            self.make, self.lo, self.hi, self.received = make, lo, hi, False

        def each(self, act, landed=False):
            def one(t, _):
                src, dst, ss, rs, dev = self.make(t, landed)
                act(
                    pltpu.make_async_remote_copy(
                        src_ref=src, dst_ref=dst, send_sem=ss, recv_sem=rs,
                        device_id=dev, device_id_type=MESH,
                    )
                )
                return 0

            if self.hi - self.lo == 1:
                one(self.lo, 0)
            else:
                lax.fori_loop(self.lo, self.hi, one, 0)

        def start(self):
            started.append(self)
            self.each(lambda c: c.start())
            return self

        def wait(self):
            self.received = True
            self.each(lambda c: c.wait_recv(), True)

        def sent(self):
            self.each(lambda c: c.wait_send())

    def finish():
        for c in started:
            if not c.received:
                c.wait()
        for c in started:
            c.sent()

    barrier = pltpu.get_barrier_semaphore()

    def greet_ctx(t, _):
        pl.semaphore_signal(barrier, inc=1, device_id=(dp, ctx_peer(t)), device_id_type=MESH)
        return 0

    def greet_plane(t, _):
        pl.semaphore_signal(
            barrier, inc=1, device_id=(zl * PLANE + plane_peer(t), ctx), device_id_type=MESH
        )
        return 0

    def greet_column(t, _):
        pl.semaphore_signal(
            barrier, inc=1, device_id=((1 - zl) * PLANE + yx, t * 2 + core), device_id_type=MESH
        )
        return 0

    lax.fori_loop(1, 8, greet_ctx, 0)
    lax.fori_loop(1, 16, greet_plane, 0)
    lax.fori_loop(0, 4, greet_column, 0)

    normed, _ = normalize(x_ref[...].astype(F32))
    xg[ctx] = normed.astype(BF16)
    for part in range(4):
        at = pl.multiple_of(part * D + ctx * HD, HD)
        wa[zl, :, part * HD:(part + 1) * HD] = win_ref[:, pl.ds(at, HD)]
    wb[zl] = wout_ref[:, pl.ds(pl.multiple_of(core * 512, 512), 512)]

    pl.semaphore_wait(barrier, 26)

    other = ((1 - zl) * PLANE + yx, ctx)

    def across(ref, k):
        return Copies(lambda t, landed: (
            ref.at[zl], ref.at[1 - zl if landed else zl], was.at[k], war.at[k], other))

    def half_rows(r, h):
        return xg.at[r, pl.ds(h * 64, 64)]

    def own_rows(s, h):
        src = ((zh + 4 - s) % 4) * 2 + core
        return Copies(lambda t, landed: (
            half_rows(ctx, h), half_rows(src if landed else ctx, h), xs.at[s * 2 + h], xr.at[s * 2 + h],
            (dp, ((zh + s) % 4) * 2 + core)))

    def relayed_rows(s, h):
        src = ((zh + 4 - s) % 4) * 2 + core
        far = ((zh + 2) % 4) * 2 + core
        return Copies(lambda t, landed: (
            half_rows(src, h), half_rows(far if landed else src, h), xs.at[4 + h], xr.at[4 + h],
            (dp, ((zh + s) % 4) * 2 + core)))

    def mate_rows(s, h):
        chip = ((zh + 4 - s) % 4) * 2
        return Copies(lambda t, landed: (
            half_rows(chip + core, h), half_rows(chip + (1 - core if landed else core), h),
            xfs.at[s * 2 + h], xfr.at[s * 2 + h], mate))

    def over_plane(src, dst, l, base):
        return Copies(lambda t, landed: (
            src.at[l], dst.at[l, plane_from(t) if landed else yx], wps.at[base + t], wpr.at[base + t],
            (zl * PLANE + plane_peer(t), ctx)), 1, PLANE)

    def from_ctx(t):
        return (ctx + 8 - t) % 8

    def all_to_all(src, dst, ss, rs):
        return Copies(lambda t, landed: (
            src.at[ctx_peer(t)], dst.at[from_ctx(t) if landed else ctx], ss.at[t], rs.at[t],
            (dp, ctx_peer(t))), 1, 8)

    xb = across(wb, 1).start()
    xa = across(wa, 0).start()
    to_mate_rows = [[None, None] for _ in range(4)]
    for h in range(2):
        to_mate_rows[0][h] = mate_rows(0, h).start()
    up0, down1 = own_rows(1, 0).start(), own_rows(3, 1).start()
    up1, down0 = own_rows(1, 1).start(), own_rows(3, 0).start()
    out_own = over_plane(wb, wrb.at[core], zl, 0).start()
    in_own = over_plane(wa, wra, zl, 32).start()

    buckets = buckets_ref[...]
    table = jnp.zeros((1, SEQ), F32)
    for b in range(32):
        table = jnp.where(buckets == b, bias_ref[ctx, b], table)
    padded = jnp.concatenate([table[:, 0:BLK], table], axis=1)
    for d in range(NBLK):
        wide = jnp.broadcast_to(padded[:, d * BLK:d * BLK + 2 * BLK], (BLK, 2 * BLK))
        toep[d] = pltpu.roll(wide, 0, 1, stride=1, stride_axis=0)[:, BLK:]

    xb.wait()
    out_other = over_plane(wb, wrb.at[core], 1 - zl, 16).start()
    wrb[core, :, yx] = wb[...]
    xa.wait()
    in_other = over_plane(wa, wra, 1 - zl, 48).start()
    wra[:, yx] = wa[...]

    up0.wait()
    far0 = relayed_rows(1, 0).start()
    to_mate_rows[1][0] = mate_rows(1, 0).start()
    down1.wait()
    far1 = relayed_rows(3, 1).start()
    to_mate_rows[3][1] = mate_rows(3, 1).start()
    up1.wait()
    to_mate_rows[1][1] = mate_rows(1, 1).start()
    down0.wait()
    to_mate_rows[3][0] = mate_rows(3, 0).start()

    out_own.wait()
    out_other.wait()
    mates_half = Copies(lambda t, landed: (
        wrb.at[core], wrb.at[1 - core if landed else core], wos.at[0], wor.at[0], mate)).start()
    in_own.wait()
    in_other.wait()
    mates_half.wait()
    ctv = ct_ref[...]
    dgt = (
        nt(wrb[0].reshape(D, 512), ctv[:, 0:512]) + nt(wrb[1].reshape(D, 512), ctv[:, 512:])
    ).astype(BF16)
    for h in range(HEADS):
        dgs[h] = dgt[h * HD:(h + 1) * HD]
    dg_sent = all_to_all(dgs, dgr, dss, dsr).start()
    dgr[ctx] = dgs[ctx]

    for part in range(4):
        piece = wra[:, :, :, part * HD:(part + 1) * HD].reshape(D, HD)
        wct[part * HD:(part + 1) * HD, :] = piece.T

    def project(zb):
        rows = xg[pl.ds(zb * 2, 2)].reshape(BLK, D)
        pre = nt(wct[...], rows)
        pret[zb] = pre
        acts = (pre * sigmoid(pre)).astype(BF16)
        actt[zb] = acts
        vrow[zb] = acts[HD:2 * HD].T
        krow[zb] = acts[3 * HD:].T

    for s in (0, 1, 3):
        for h in range(2):
            to_mate_rows[s][h].wait()
        project((zh + 4 - s) % 4)
    far0.wait()
    to_mate_rows[2][0] = mate_rows(2, 0).start()
    far1.wait()
    to_mate_rows[2][1] = mate_rows(2, 1).start()
    for h in range(2):
        to_mate_rows[2][h].wait()
    project((zh + 2) % 4)

    l0, l1, l2 = lengths_ref[0, 0], lengths_ref[0, 1], lengths_ref[0, 2]
    e0, e1, e2 = l0, l0 + l1, l0 + l1 + l2

    def pair_of(p):
        i = (p >= 1).astype(jnp.int32) + (p >= 3).astype(jnp.int32) + (p >= 6).astype(jnp.int32)
        return i, p - (i * (i + 1)) // 2

    def dg_block(b):
        return jnp.concatenate([dgr[2 * b], dgr[2 * b + 1]], axis=1).astype(F32)

    def forward(i):
        qpos = i * BLK + lax.broadcasted_iota(jnp.int32, (1, BLK), 1)
        first = jnp.where(qpos >= e2, e2, jnp.where(qpos >= e1, e1, jnp.where(qpos >= e0, e0, 0)))
        att = jnp.zeros((HD, BLK), F32)
        for j in range(i + 1):
            p = i * (i + 1) // 2 + j
            scores = nn(krow[j], actt[i, 2 * HD:3 * HD, :]) * SCALE + toep[i - j]
            kpos = j * BLK + lax.broadcasted_iota(jnp.int32, (BLK, BLK), 0)
            allowed = kpos >= first
            if i == j:
                allowed = allowed & (kpos <= qpos)
            sig = sigmoid(scores)
            act = scores * sig
            weights = jnp.where(allowed, act * (1.0 / SEQ), 0.0).astype(BF16)
            wts[p] = weights
            sgs[p] = jnp.where(allowed, (sig + act * (1.0 - sig)) * (1.0 / SEQ), 0.0)
            att = att + nn(actt[j, HD:2 * HD, :], weights)
        attt[i] = att

    def statistics(b):
        att = attt[b]
        up = dg_block(b) * actt[b, 0:HD, :].astype(F32)
        mean = jnp.sum(att, axis=0, keepdims=True) * (1.0 / HD)
        cen = att - mean
        rows = [
            mean,
            jnp.sum(cen * cen, axis=0, keepdims=True),
            jnp.sum(up, axis=0, keepdims=True),
            jnp.sum(up * cen, axis=0, keepdims=True),
        ]
        stat[b] = jnp.concatenate([q[:, :ROWS] for q in rows] + [q[:, ROWS:] for q in rows], axis=0)
        statr[b, ctx] = stat[b]
        return Copies(lambda t, landed: (
            stat.at[b], statr.at[b, from_ctx(t) if landed else ctx], sts.at[b * 8 + t], strr.at[b * 8 + t],
            (dp, ctx_peer(t))), 1, 8).start()

    stats_sent = {}
    for b in (3, 2, 1, 0):
        forward(b)
        if b == 3:
            dg_sent.wait()
        stats_sent[b] = statistics(b)

    dqt[...] = jnp.zeros_like(dqt)
    dkt[...] = jnp.zeros_like(dkt)
    dvt[...] = jnp.zeros_like(dvt)
    def combined(b):
        stats_sent[b].wait()
        parts = [
            jnp.concatenate([statr[b, r, 0:4], statr[b, r, 4:8]], axis=1) for r in range(HEADS)
        ]
        mean = sum([q[0:1] for q in parts]) * (1.0 / HEADS)
        var, s3, s4 = 0.0, 0.0, 0.0
        for q in parts:
            off = q[0:1] - mean
            var = var + q[1:2] + HD * off * off
            s3 = s3 + q[2:3]
            s4 = s4 + q[3:4] + off * q[2:3]
        inv = lax.rsqrt(var * (1.0 / D) + EPSILON)
        m1 = s3 * (1.0 / D)
        m2 = s4 * inv * (1.0 / D)
        norm = (attt[b] - mean) * inv
        dg = dg_block(b)
        u = actt[b, 0:HD, :].astype(F32)
        gated = (norm * u).astype(BF16)
        gts[2 * b] = gated[:, 0:ROWS]
        gts[2 * b + 1] = gated[:, ROWS:]
        dat[b] = ((dg * u - m1 - norm * m2) * inv).astype(BF16)
        uf[b] = dg * norm

    for b in (3, 2, 1, 0):
        combined(b)
    gated_sent = all_to_all(gts, gtr, gss, gsr).start()
    gtr[ctx] = gts[ctx]

    def backward(p, _):
        i, j = pair_of(p)
        da = dat[i]
        ds = (nn(vrow[j], da) * sgs[p]).astype(BF16)
        dqt[i] += nn(actt[j, 3 * HD:, :], ds)
        dkt[j] += nt(actt[i, 2 * HD:3 * HD, :], ds)
        dvt[j] += nt(da, wts[p])
        return 0

    lax.fori_loop(0, PAIRS, backward, 0)

    for b in range(NBLK):
        for part, val in enumerate((uf[b], dvt[b], dqt[b] * SCALE, dkt[b] * SCALE)):
            pre = pret[b, part * HD:(part + 1) * HD, :]
            sig = sigmoid(pre)
            dpt[b, part * HD:(part + 1) * HD, :] = (
                val * (sig * (1.0 + pre * (1.0 - sig)))
            ).astype(BF16)

    def to_mate(b):
        return Copies(lambda t, landed: (pd.at[b], pdr.at[b], pds.at[b], pdsr.at[b], mate))

    mates = {}
    for s in (2, 1, 3, 0):
        b = (zh + s) % 4
        col = pl.multiple_of((1 - core) * ROWS, ROWS)
        pd[b] = tn(dpt[b, :, pl.ds(col, ROWS)], wct[...]).astype(BF16)
        mates[s] = to_mate(b).start()

    def to_owner(s):
        return Copies(lambda t, landed: (
            ps.at[s], pr.at[s], pss.at[s], psr.at[s], (dp, ((zh + s) % 4) * 2 + core)))

    owners = {}

    for s in (2, 1, 3, 0):
        b = (zh + s) % 4
        col = pl.multiple_of(core * ROWS, ROWS)
        mine = tn(dpt[b, :, pl.ds(col, ROWS)], wct[...])
        mates[s].wait()
        both = mine + pdr[b].astype(F32)
        if s:
            ps[s] = both.astype(BF16)
            owners[s] = to_owner(s).start()
        else:
            own[...] = both

    gated_sent.wait()
    gt = gtr[...].reshape(D, ROWS)
    for half in range(2):
        cols = slice(half * 512, half * 512 + 512)
        out_ref[:, cols] = (
            x_ref[:, cols].astype(F32) + tn(gt, wrb[half].reshape(D, 512))
        ).astype(BF16)

    def ct_cols(which):
        return jnp.concatenate(
            [ct_ref[:, pl.ds(pl.multiple_of(b * BLK + which * HD, HD), HD)] for b in range(NBLK)], axis=1
        )

    wgd[...] = nn(gt, ct_cols(1 - core)).astype(BF16)
    wg_mate = Copies(lambda t, landed: (wgd, wgdr, wds.at[0], wdr.at[0], mate)).start()
    wmine = nn(gt, ct_cols(core))
    wg_mate.wait()
    wgs[...] = (wmine + wgdr[...].astype(F32)).astype(BF16).reshape(2, PLANE, 32, 512)

    wg_plane = Copies(lambda t, landed: (
        wgs.at[:, plane_peer(t)], wgr.at[plane_from(t) if landed else yx], wgss.at[t], wgsr.at[t],
        (zl * PLANE + plane_peer(t), ctx)), 1, PLANE).start()
    wgr[yx] = wgs[:, yx]
    wg_plane.wait()

    def add_plane(t, total):
        return total + wgr[t].astype(F32)

    wsum = lax.fori_loop(0, PLANE, add_plane, jnp.zeros((2, 32, 512), F32)).astype(BF16)
    for l in range(2):
        for h in range(4):
            wzs[l * 4 + h] = wsum[l, :, h * HD:(h + 1) * HD]

    zat = zl * 4 + zh

    def column(t, landed):
        to = (zat + t) % 8
        return (
            wzs.at[to], wzr.at[(zat + 8 - t) % 8 if landed else zat], wzss.at[t], wzsr.at[t],
            ((to // 4) * PLANE + yx, (to % 4) * 2 + core),
        )

    wg_column = Copies(column, 1, 8).start()
    wzr[zat] = wzs[zat]

    total = own[...]
    for s in (1, 3, 2):
        owners[s].wait()
        total = total + pr[s].astype(F32)
    normed, inverse = normalize(x_ref[...].astype(F32))
    first = jnp.mean(total, axis=-1, keepdims=True)
    second = jnp.mean(total * normed, axis=-1, keepdims=True)
    grads_ref[...] = (
        ct_ref[...].astype(F32) + (total - first - normed * second) * inverse
    ).astype(BF16)

    wg_column.wait()
    wg_ref[...] = jnp.sum(wzr[...].astype(F32), axis=0)

    finish()


def on_device(inputs, input_weight, output_weight, cotangent, lengths, buckets, bias_weights):
    vm = lambda *shape, dt=BF16: pltpu.VMEM(shape, dt)
    sem = lambda n: pltpu.SemaphoreType.DMA((n,))
    scratch = [
        vm(8, ROWS, D), vm(2, 32, 512), vm(2, 32, 512),
        vm(2, PLANE, 32, 512), vm(2, 2, PLANE, 32, 512),
        vm(512, D), vm(NBLK, 512, BLK, dt=F32), vm(NBLK, 512, BLK),
        vm(NBLK, BLK, HD), vm(NBLK, BLK, HD),
        vm(PAIRS, BLK, BLK), vm(PAIRS, BLK, BLK, dt=F32), vm(NBLK, BLK, BLK, dt=F32),
        vm(NBLK, HD, BLK, dt=F32), vm(NBLK, HD, BLK, dt=F32),
        vm(8, HD, ROWS), vm(8, HD, ROWS),
        vm(NBLK, 8, HD, dt=F32), vm(NBLK, 8, 8, HD, dt=F32),
        vm(8, HD, ROWS), vm(8, HD, ROWS), vm(NBLK, HD, BLK),
        vm(NBLK, HD, BLK, dt=F32), vm(NBLK, HD, BLK, dt=F32), vm(NBLK, HD, BLK, dt=F32),
        vm(NBLK, 512, BLK),
        vm(D, 512), vm(D, 512), vm(2, PLANE, 32, 512), vm(PLANE, 2, 32, 512),
        vm(8, 32, HD), vm(8, 32, HD),
        vm(NBLK, ROWS, D), vm(NBLK, ROWS, D), vm(4, ROWS, D), vm(4, ROWS, D), vm(ROWS, D, dt=F32),
        sem(8), sem(8), sem(8), sem(8), sem(2), sem(2), sem(64), sem(64), sem(1), sem(1),
        sem(8), sem(8), sem(32), sem(32), sem(8), sem(8),
        sem(1), sem(1), sem(16), sem(16), sem(8), sem(8), sem(4), sem(4), sem(4), sem(4),
    ]
    vspec = pl.BlockSpec(memory_space=pltpu.VMEM)
    sspec = pl.BlockSpec(memory_space=pltpu.SMEM)
    return pl.pallas_call(
        kernel,
        name="hstu",
        out_shape=(
            jax.ShapeDtypeStruct((ROWS, D), BF16),
            jax.ShapeDtypeStruct((ROWS, D), BF16),
            jax.ShapeDtypeStruct((32, HD), F32),
        ),
        in_specs=[sspec, sspec, vspec, vspec, vspec, vspec, vspec],
        out_specs=(vspec, vspec, vspec),
        scratch_shapes=scratch,
        compiler_params=pltpu.CompilerParams(
            collective_id=0, has_side_effects=True, vmem_limit_bytes=56 << 20
        ),
    )(lengths, bias_weights, buckets.reshape(1, SEQ), inputs, input_weight, output_weight, cotangent)


def solution(mesh):
    return jax.shard_map(
        on_device,
        mesh=mesh,
        in_specs=(
            P(("dp", "ctx"), None),
            P("dp", None),
            P("dp", None),
            P(("dp", "ctx"), None),
            P("dp", None),
            P(),
            P(),
        ),
        out_specs=(P(("dp", "ctx"), None), P(("dp", "ctx"), None), P("dp", "ctx")),
        check_vma=False,
    )
```

time: 116 us -> 96.1 us (0.83)
  Pallas kernels: 112 us -> 92.3 us
    pallas_call x1, Pallas kernels: 112 us -> 92.3 us  [on_device(): pl.pallas_call(kernel, name='hstu', out_shape=(jax.ShapeDtypeStruct((ROWS...]
where the time goes in v2:
time: 96.1 us; the launch traced here: 96 us
  Pallas kernels  92.3 us (96%)
  local copies, waits for them, and re-layouts  3.04 us (3%)
    pallas_call x1, Pallas kernels, on_device(): pl.pallas_call(kernel, name='hstu', out_shape=(jax.ShapeDtypeStruct((ROWS...  92.3 us
    unnamed x7, local copies, waits for them, and re-layouts  3.04 us

profile of v2, /device:TPU:1, one launch (start us, length us, event | category | flops | bytes accessed | tf_op | source)
XLA Modules:
  0.0 96.0 jit_solution(8284985288097659070)
XLA Ops:
  0.6 92.3 %hstu.1 = (bf16[128,1024]{1,0:T(8,128)(2,1)}, bf16[128,1024]{1,0:T(8,128)(2,1)}, f32[32,128]{1,0:T(8,128)}) custom-call(s32[1,4]{1,0:T(1,128)} %lengths_ref.1, f32[8,32]{1,0:T(8,128)} %bias_ref.1, s32[1,1024]{1,0:T(1,128)} %bitcast.1, bf16[128,1024]{1,0:T(8,128)(2,1)} %x_ref.1, bf16[32,4096]{1,0:T(8,128)(2,1)} %win_ref.1, bf16[32,1024]{1,0:T(8,128)(2,1)} %wout_ref.1, ...), custom_call_target="tpu_custom_call" | custom-call | tf_op jit(solution)/shard_map/hstu/pallas_call | solution.py:486
  92.9 0.0 copy-start
  92.9 1.7 %copy.13 = bf16[128,1024]{1,0:T(8,128)(2,1)} copy(bf16[128,1024]{1,0:T(8,128)(2,1)} %get-tuple-element.6) | data formatting | bytes 524288
  94.6 0.0 copy-done
  94.6 0.0 copy-start.1
  94.6 0.7 copy.14
  95.3 0.0 copy-done.1
  95.3 0.6 copy.15
Async XLA Ops:
  92.9 1.7 %copy-start = (bf16[128,1024]{1,0:T(8,128)(2,1)S(1)}, bf16[128,1024]{1,0:T(8,128)(2,1)}, u32[]{:S(2)}) copy-start(bf16[128,1024]{1,0:T(8,128)(2,1)} %get-tuple-element.7) | copy-start | bytes 786436
  94.6 0.7 copy-start.1

commit v3 on v2

v3 whole, which is shorter than its diff:
```python
import functools
import math

import jax
import jax.numpy as jnp
from jax import lax
from jax.experimental import pallas as pl
from jax.experimental.pallas import tpu as pltpu
from jax.sharding import PartitionSpec as P

EPSILON = 1e-06
MESH = pl.DeviceIdType.MESH
F32 = jnp.float32
BF16 = jnp.bfloat16

ROWS = 128
BLK = 256
NBLK = 4
HEADS = 8
HD = 128
D = 1024
SEQ = 1024
PLANE = 16
PAIRS = NBLK * (NBLK + 1) // 2
SCALE = 1.0 / math.sqrt(HD)


def nn(a, b):
    return lax.dot_general(a, b, (((1,), (0,)), ((), ())), preferred_element_type=F32)


def nt(a, b):
    return lax.dot_general(a, b, (((1,), (1,)), ((), ())), preferred_element_type=F32)


def tn(a, b):
    return lax.dot_general(a, b, (((0,), (0,)), ((), ())), preferred_element_type=F32)


def sigmoid(values):
    return 0.5 * jnp.tanh(0.5 * values) + 0.5


def normalize(values):
    average = jnp.mean(values, axis=-1, keepdims=True)
    centered = values - average
    inverse = lax.rsqrt(jnp.mean(centered * centered, axis=-1, keepdims=True) + EPSILON)
    return (centered * inverse, inverse)


def kernel(
    lengths_ref, bias_ref, buckets_ref, x_ref, win_ref, wout_ref, ct_ref,
    out_ref, grads_ref, wg_ref,
    xg, wa, wb, wbo, wra, wrb, wct, pret, actt, krow, vrow, wts, sgs, toep, attt, uf,
    dgs, dgr, stat, statr, ats, atr, uts, utr, gto, gtm, ctc, xv, dat, dkt, dvt, dpt,
    wgs, wgr, wzs, wzr,
    pd, pdr, pm, ps, pr, rr, own,
    xs, xr, xfs, xfr, was, war, wps, wpr, wos, wor, dss, dsr, sts, strr, gss, gsr,
    wds, wdr, wgss, wgsr, wzss, wzsr, pds, pdsr, pss, psr, uss, usr, lds,
):
    dp = lax.axis_index("dp")
    ctx = lax.axis_index("ctx")
    zh, core = ctx // 2, ctx % 2
    zl, yx = dp // PLANE, dp % PLANE
    y, x = yx // 4, yx % 4
    mate = (dp, zh * 2 + 1 - core)

    def ctx_peer(t):
        return (ctx + t) % 8

    def plane_peer(t):
        return ((y + t // 4) % 4) * 4 + (x + t % 4) % 4

    def plane_from(t):
        return ((y + 4 - t // 4) % 4) * 4 + (x + 4 - t % 4) % 4

    started = []

    class Copies:
        def __init__(self, make, lo=0, hi=1, where=None):
            self.make, self.lo, self.hi, self.where, self.received = make, lo, hi, where, False

        def each(self, act, landed=False):
            def one(t, _):
                if self.where is None:
                    run(t)
                else:
                    pl.when(self.where(t, landed))(lambda: run(t))
                return 0

            def run(t):
                src, dst, ss, rs, dev = self.make(t, landed)
                act(
                    pltpu.make_async_remote_copy(
                        src_ref=src, dst_ref=dst, send_sem=ss, recv_sem=rs,
                        device_id=dev, device_id_type=MESH,
                    )
                )

            if self.hi - self.lo == 1:
                one(self.lo, 0)
            else:
                lax.fori_loop(self.lo, self.hi, one, 0)

        def go(self):
            self.each(lambda c: c.start())

        def start(self):
            started.append(self)
            self.go()
            return self

        def wait(self):
            self.received = True
            self.each(lambda c: c.wait_recv(), True)

        def sent(self):
            self.each(lambda c: c.wait_send())

    def finish():
        for c in started:
            if not c.received:
                c.wait()
        for c in started:
            c.sent()

    barrier = pltpu.get_barrier_semaphore()

    def greet_ctx(t, _):
        pl.semaphore_signal(barrier, inc=1, device_id=(dp, ctx_peer(t)), device_id_type=MESH)
        return 0

    def greet_plane(t, _):
        pl.semaphore_signal(
            barrier, inc=1, device_id=(zl * PLANE + plane_peer(t), ctx), device_id_type=MESH
        )
        return 0

    def greet_column(t, _):
        pl.semaphore_signal(
            barrier, inc=1, device_id=((1 - zl) * PLANE + yx, t * 2 + core), device_id_type=MESH
        )
        return 0

    lax.fori_loop(1, 8, greet_ctx, 0)
    lax.fori_loop(1, 16, greet_plane, 0)
    lax.fori_loop(0, 4, greet_column, 0)

    load_x = pltpu.make_async_copy(x_ref, xv, lds.at[0])
    load_x.start()
    load_w = [
        pltpu.make_async_copy(wout_ref, wbo, lds.at[1])
    ]
    for part in range(4):
        at = pl.multiple_of(part * D + ctx * HD, HD)
        load_w.append(
            pltpu.make_async_copy(
                win_ref.at[:, pl.ds(at, HD)], wa.at[zl, :, pl.ds(part * HD, HD)], lds.at[2 + part]
            )
        )
    for c in load_w:
        c.start()
    load_ct = pltpu.make_async_copy(ct_ref, ctc.at[core], lds.at[6])
    load_ct.start()
    load_x.wait()
    normed, _ = normalize(xv[...].astype(F32))
    xg[ctx] = normed.astype(BF16)
    for c in load_w:
        c.wait()

    pl.semaphore_wait(barrier, 26)

    other = ((1 - zl) * PLANE + yx, ctx)

    def across(ref, k):
        return Copies(lambda t, landed: (
            ref.at[zl], ref.at[1 - zl if landed else zl], was.at[k], war.at[k], other))

    def half_rows(r, h):
        return xg.at[r, pl.ds(h * 64, 64)]

    def own_rows(s, h):
        src = ((zh + 4 - s) % 4) * 2 + core
        return Copies(lambda t, landed: (
            half_rows(ctx, h), half_rows(src if landed else ctx, h), xs.at[s * 2 + h], xr.at[s * 2 + h],
            (dp, ((zh + s) % 4) * 2 + core)))

    def relayed_rows(s, h):
        src = ((zh + 4 - s) % 4) * 2 + core
        far = ((zh + 2) % 4) * 2 + core
        return Copies(lambda t, landed: (
            half_rows(src, h), half_rows(far if landed else src, h), xs.at[4 + h], xr.at[4 + h],
            (dp, ((zh + s) % 4) * 2 + core)))

    def mate_rows(s, h):
        chip = ((zh + 4 - s) % 4) * 2
        return Copies(lambda t, landed: (
            half_rows(chip + core, h), half_rows(chip + (1 - core if landed else core), h),
            xfs.at[s * 2 + h], xfr.at[s * 2 + h], mate))

    def step_by(axis, ty, tx, t):
        return (ty, (tx + t) % 4) if axis == "x" else ((ty + t) % 4, tx)

    def in_plane(place):
        return (zl * PLANE + place[0] * 4 + place[1], ctx)

    class Spread:
        def __init__(self, src, dst, axis, base):
            self.src, self.dst, self.axis, self.base = src, dst, axis, base
            self.cross = "y" if axis == "x" else "x"
            self.first, self.rest = [], []

        def own(self):
            for axis in (self.axis, self.cross):
                for t in (1, 3, 2):
                    at = self.base + (axis == self.cross) * 3 + t - 1

                    def make(_, landed, axis=axis, t=t, at=at):
                        py, px = step_by(axis, y, x, 4 - t) if landed else (y, x)
                        return (self.src, self.dst(py, px), wps.at[at], wpr.at[at],
                                in_plane(step_by(axis, y, x, t)))

                    (self.first if axis == self.axis else self.rest).append(Copies(make).start())

        def hand_on(self):
            for n, t in enumerate((1, 3, 2)):
                self.first[n].wait()
                for u in (1, 3, 2):
                    at = self.base + 6 + (t - 1) * 3 + u - 1

                    def make(_, landed, t=t, u=u, at=at):
                        py, px = step_by(self.axis, y, x, 4 - t)
                        ty, tx = step_by(self.cross, py, px, 4 - u) if landed else (py, px)
                        return (self.dst(py, px), self.dst(ty, tx), wps.at[at], wpr.at[at],
                                in_plane(step_by(self.cross, y, x, u)))

                    self.rest.append(Copies(make).start())

        def wait(self):
            for c in self.rest:
                c.wait()

    def from_ctx(t):
        return (ctx + 8 - t) % 8

    def all_to_all(src, dst, ss, rs):
        return Copies(lambda t, landed: (
            src.at[ctx_peer(t)], dst.at[from_ctx(t) if landed else ctx], ss.at[t], rs.at[t],
            (dp, ctx_peer(t))), 1, 8)

    mine_b = zl == core
    xb = Copies(lambda t, landed: (wbo, wb, was.at[1], war.at[1], other), where=lambda t, landed: (
        jnp.logical_not(mine_b) if landed else mine_b)).start()
    xa = across(wa, 0).start()
    to_mate_rows = [[None, None] for _ in range(4)]
    for h in range(2):
        to_mate_rows[0][h] = mate_rows(0, h).start()
    up0, down1 = own_rows(1, 0).start(), own_rows(3, 1).start()
    up1, down0 = own_rows(1, 1).start(), own_rows(3, 0).start()
    @pl.when(mine_b)
    def _():
        wb[...] = wbo[...]

    xb.wait()
    lo, hi = pl.ds(0, 512), pl.ds(512, 512)
    out_spread = [
        Spread(wb.at[:, lo], lambda py, px: wrb.at[core, py, px, :, lo], "x", 0),
        Spread(wb.at[:, hi], lambda py, px: wrb.at[core, py, px, :, hi], "y", 16),
    ]
    for w in out_spread:
        w.own()
    load_ct.wait()
    ct_mate = Copies(lambda t, landed: (
        ctc.at[core], ctc.at[1 - core if landed else core], wds.at[0], wdr.at[0], mate)).start()
    xa.wait()
    low, high = pl.ds(0, 256), pl.ds(256, 256)
    in_spread = [
        Spread(wa.at[:, :, low], lambda py, px: wra.at[:, py, px, :, low], "x", 32),
        Spread(wa.at[:, :, high], lambda py, px: wra.at[:, py, px, :, high], "y", 48),
    ]
    for w in in_spread:
        w.own()
    wrb[core, y, x] = wb[...]
    wra[:, y, x] = wa[...]
    for w in out_spread:
        w.hand_on()

    buckets = buckets_ref[...]
    table = jnp.zeros((1, SEQ), F32)
    for b in range(32):
        table = jnp.where(buckets == b, bias_ref[ctx, b], table)
    padded = jnp.concatenate([table[:, 0:BLK], table], axis=1)
    for d in range(NBLK):
        wide = jnp.broadcast_to(padded[:, d * BLK:d * BLK + 2 * BLK], (BLK, 2 * BLK))
        toep[d] = pltpu.roll(wide, 0, 1, stride=1, stride_axis=0)[:, BLK:]

    up0.wait()
    far0 = relayed_rows(1, 0).start()
    to_mate_rows[1][0] = mate_rows(1, 0).start()
    down1.wait()
    far1 = relayed_rows(3, 1).start()
    to_mate_rows[3][1] = mate_rows(3, 1).start()
    up1.wait()
    to_mate_rows[1][1] = mate_rows(1, 1).start()
    down0.wait()
    to_mate_rows[3][0] = mate_rows(3, 0).start()

    for w in in_spread:
        w.hand_on()

    for w in out_spread:
        w.wait()
    ct_mate.wait()
    ct_chip = ctc[...].reshape(BLK, D)
    wout_half = wrb[core].reshape(512, D)
    for n in range(4):
        dgs[n] = nt(wout_half[n * HD:(n + 1) * HD], ct_chip).astype(BF16)

    def head_at(n):
        return core * 4 + n

    from_half = zh // 2
    dg_sent = Copies(
        lambda t, landed: (
            dgs.at[t], dgr.at[t if landed else zh], dss.at[t], dsr.at[t if landed else zh], (dp, head_at(t))),
        0, 4,
        where=lambda t, landed: (t * 2 + from_half != ctx) if landed else (head_at(t) != ctx),
    ).start()

    @pl.when(from_half == core)
    def _():
        dgr[zh] = dgs[ctx % 4]

    mates_half = Copies(lambda t, landed: (
        wrb.at[core], wrb.at[1 - core if landed else core], wos.at[0], wor.at[0], mate)).start()

    for w in in_spread:
        w.wait()
    for part in range(4):
        piece = wra[:, :, :, :, part * HD:(part + 1) * HD].reshape(D, HD)
        wct[part * HD:(part + 1) * HD, :] = piece.T

    def project(zb):
        rows = xg[pl.ds(zb * 2, 2)].reshape(BLK, D)
        pre = nt(wct[...], rows)
        pret[zb] = pre
        acts = (pre * sigmoid(pre)).astype(BF16)
        actt[zb] = acts
        vrow[zb] = acts[HD:2 * HD].T
        krow[zb] = acts[3 * HD:].T

    for s in (0, 1, 3):
        for h in range(2):
            to_mate_rows[s][h].wait()
        project((zh + 4 - s) % 4)
    far0.wait()
    to_mate_rows[2][0] = mate_rows(2, 0).start()
    far1.wait()
    to_mate_rows[2][1] = mate_rows(2, 1).start()
    for h in range(2):
        to_mate_rows[2][h].wait()
    project((zh + 2) % 4)

    for b in range(NBLK):
        uts[2 * b] = actt[b, 0:HD, 0:ROWS]
        uts[2 * b + 1] = actt[b, 0:HD, ROWS:]
    u_sent = all_to_all(uts, utr, uss, usr).start()
    utr[ctx] = uts[ctx]

    l0, l1, l2 = lengths_ref[0, 0], lengths_ref[0, 1], lengths_ref[0, 2]
    e0, e1, e2 = l0, l0 + l1, l0 + l1 + l2

    def forward(i):
        qpos = i * BLK + lax.broadcasted_iota(jnp.int32, (1, BLK), 1)
        first = jnp.where(qpos >= e2, e2, jnp.where(qpos >= e1, e1, jnp.where(qpos >= e0, e0, 0)))
        att = jnp.zeros((HD, BLK), F32)
        for j in range(i + 1):
            p = i * (i + 1) // 2 + j
            scores = nn(krow[j], actt[i, 2 * HD:3 * HD, :]) * SCALE + toep[i - j]
            kpos = j * BLK + lax.broadcasted_iota(jnp.int32, (BLK, BLK), 0)
            allowed = kpos >= first
            if i == j:
                allowed = allowed & (kpos <= qpos)
            sig = sigmoid(scores)
            act = scores * sig
            weights = jnp.where(allowed, act * (1.0 / SEQ), 0.0).astype(BF16)
            wts[p] = weights
            sgs[p] = jnp.where(allowed, (sig + act * (1.0 - sig)) * (1.0 / SEQ), 0.0)
            att = att + nn(actt[j, HD:2 * HD, :], weights)
        attt[i] = att

    def statistics(b):
        att = attt[b]
        up = dgr[b].astype(F32) * actt[b, 0:HD, :].astype(F32)
        mean = jnp.sum(att, axis=0, keepdims=True) * (1.0 / HD)
        cen = att - mean
        ats[2 * b] = cen[:, 0:ROWS].astype(BF16)
        ats[2 * b + 1] = cen[:, ROWS:].astype(BF16)
        rows = [
            mean,
            jnp.sum(cen * cen, axis=0, keepdims=True),
            jnp.sum(up, axis=0, keepdims=True),
            jnp.sum(up * cen, axis=0, keepdims=True),
        ]
        stat[b] = jnp.concatenate([q[:, :ROWS] for q in rows] + [q[:, ROWS:] for q in rows], axis=0)

    for b in (3, 2, 1, 0):
        forward(b)
    dg_sent.wait()
    for b in (3, 2, 1, 0):
        statistics(b)
    stats_sent = Copies(lambda t, landed: (
        stat, statr.at[from_ctx(t) if landed else ctx], sts.at[t], strr.at[t], (dp, ctx_peer(t))), 1, 8).start()
    statr[ctx] = stat[...]
    att_sent = all_to_all(ats, atr, gss, gsr).start()
    atr[ctx] = ats[ctx]

    def combined(b):
        parts = [
            jnp.concatenate([statr[r, b, 0:4], statr[r, b, 4:8]], axis=1) for r in range(HEADS)
        ]
        mean = sum([q[0:1] for q in parts]) * (1.0 / HEADS)
        var, s3, s4 = 0.0, 0.0, 0.0
        for q in parts:
            off = q[0:1] - mean
            var = var + q[1:2] + HD * off * off
            s3 = s3 + q[2:3]
            s4 = s4 + q[3:4] + off * q[2:3]
        inv = lax.rsqrt(var * (1.0 / D) + EPSILON)
        m1 = s3 * (1.0 / D)
        m2 = s4 * inv * (1.0 / D)
        norm = (attt[b] - mean) * inv
        dg = dgr[b].astype(F32)
        u = actt[b, 0:HD, :].astype(F32)
        dat[b] = ((dg * u - m1 - norm * m2) * inv).astype(BF16)
        uf[b] = dg * norm

    def backward(i):
        da = dat[i]
        dq = jnp.zeros((HD, BLK), F32)
        for j in range(i + 1):
            p = i * (i + 1) // 2 + j
            ds = (nn(vrow[j], da) * sgs[p]).astype(BF16)
            dq = dq + nn(actt[j, 3 * HD:, :], ds)
            dk = nt(actt[i, 2 * HD:3 * HD, :], ds)
            dv = nt(da, wts[p])
            if i < NBLK - 1:
                dk, dv = dk + dkt[j], dv + dvt[j]
            dkt[j] = dk
            dvt[j] = dv
        for part, val in enumerate((uf[i], dvt[i], dq * SCALE, dkt[i] * SCALE)):
            pre = pret[i, part * HD:(part + 1) * HD, :]
            sig = sigmoid(pre)
            dpt[i, part * HD:(part + 1) * HD, :] = (
                val * (sig * (1.0 + pre * (1.0 - sig)))
            ).astype(BF16)

    mates = {}

    def terms(b):
        theirs = pl.multiple_of((1 - core) * ROWS, ROWS)
        pd[b] = tn(dpt[b, :, pl.ds(theirs, ROWS)], wct[...]).astype(BF16)
        mates[b] = Copies(lambda t, landed: (pd.at[b], pdr.at[b], pds.at[b], pdsr.at[b], mate)).start()
        mine = pl.multiple_of(core * ROWS, ROWS)
        pm[b] = tn(dpt[b, :, pl.ds(mine, ROWS)], wct[...])

    half = (pl.ds(0, 64), pl.ds(64, 64))
    up = (dp, ((zh + 1) % 4) * 2 + core)
    down = (dp, ((zh + 3) % 4) * 2 + core)

    def round_copy(n, src, dst, to):
        return Copies(lambda t, landed: (src, dst, pss.at[n], psr.at[n], to))

    far = [
        round_copy(0, ps.at[2, half[0]], rr.at[0], up),
        round_copy(1, ps.at[2, half[1]], rr.at[1], down),
    ]
    near = {
        (1, 0): round_copy(2, ps.at[1, half[0]], pr.at[1, half[0]], up),
        (1, 1): round_copy(3, ps.at[1, half[1]], pr.at[1, half[1]], up),
        (3, 0): round_copy(4, ps.at[3, half[0]], pr.at[3, half[0]], down),
        (3, 1): round_copy(5, ps.at[3, half[1]], pr.at[3, half[1]], down),
    }
    started.extend(far)
    started.extend(near.values())

    def chip_sum(b):
        mates[b].wait()
        s = (b + 4 - zh) % 4

        @pl.when(s == 0)
        def _():
            own[...] = pm[b] + pdr[b].astype(F32)

        @pl.when(s == 2)
        def _():
            ps[2] = (pm[b] + pdr[b].astype(F32)).astype(BF16)
            far[0].go()
            far[1].go()

        @pl.when(s == 1)
        def _():
            ps[1, half[1]] = (pm[b, half[1]] + pdr[b, half[1]].astype(F32)).astype(BF16)
            near[1, 1].go()

        @pl.when(s == 3)
        def _():
            ps[3, half[0]] = (pm[b, half[0]] + pdr[b, half[0]].astype(F32)).astype(BF16)
            near[3, 0].go()

    def relay(b):
        s = (b + 4 - zh) % 4
        for n, way, h in ((0, 1, 0), (1, 3, 1)):
            @pl.when(s == way)
            def _():
                far[n].wait()
                ps[way, half[h]] = (
                    pm[b, half[h]] + pdr[b, half[h]].astype(F32) + rr[n].astype(F32)
                ).astype(BF16)
                near[way, h].go()

    stats_sent.wait()
    combined(3)
    backward(3)
    terms(3)

    u_sent.wait()
    att_sent.wait()
    mine = [jnp.where(core == 0, statr[r, zh, 0:4], statr[r, zh, 4:8]) for r in range(HEADS)]
    mean = sum([q[0:1] for q in mine]) * (1.0 / HEADS)
    var = 0.0
    for q in mine:
        off = q[0:1] - mean
        var = var + q[1:2] + HD * off * off
    inv = lax.rsqrt(var * (1.0 / D) + EPSILON)
    for r in range(HEADS):
        norm = (atr[r].astype(F32) + (mine[r][0:1] - mean)) * inv
        gto[r * HD:(r + 1) * HD] = (norm * utr[r].astype(F32)).astype(BF16)
    gated_mate = Copies(lambda t, landed: (gto, gtm, wds.at[1], wdr.at[1], mate)).start()
    combined(2)
    backward(2)
    chip_sum(3)
    terms(2)

    def ct_cols(which):
        return jnp.concatenate(
            [ctc[which, :, pl.ds(pl.multiple_of(b * BLK + core * HD, HD), HD)] for b in range(NBLK)], axis=1
        )

    gated_mate.wait()
    both = jnp.concatenate([gto[...], gtm[...]], axis=1)
    cts = jnp.concatenate([ct_cols(core), ct_cols(1 - core)], axis=0)
    wgs[...] = nn(both, cts).astype(BF16).reshape(2, PLANE, 32, 512)
    wg_plane = Copies(lambda t, landed: (
        wgs.at[:, plane_peer(t)], wgr.at[plane_from(t) if landed else yx], wgss.at[t], wgsr.at[t],
        (zl * PLANE + plane_peer(t), ctx)), 1, PLANE).start()
    wgr[yx] = wgs[:, yx]
    combined(1)
    backward(1)
    chip_sum(2)
    terms(1)
    combined(0)
    backward(0)
    chip_sum(1)
    terms(0)
    chip_sum(0)
    for b in (3, 2, 1, 0):
        relay(b)
    mates_half.wait()
    gated = gto[...]
    out_ref[...] = (
        xv[...].astype(F32)
        + tn(gated[0:512], wrb[0].reshape(512, D)) + tn(gated[512:], wrb[1].reshape(512, D))
    ).astype(BF16)

    wg_plane.wait()

    def add_plane(t, total):
        return total + wgr[t].astype(F32)

    wsum = lax.fori_loop(0, PLANE, add_plane, jnp.zeros((2, 32, 512), F32)).astype(BF16)
    for l in range(2):
        for h in range(4):
            wzs[l * 4 + h] = wsum[l, :, h * HD:(h + 1) * HD]

    zat = zl * 4 + zh

    def column(t, landed):
        to = (zat + t) % 8
        return (
            wzs.at[to], wzr.at[(zat + 8 - t) % 8 if landed else zat], wzss.at[t], wzsr.at[t],
            ((to // 4) * PLANE + yx, (to % 4) * 2 + core),
        )

    wg_column = Copies(column, 1, 8).start()
    wzr[zat] = wzs[zat]

    for c in near.values():
        c.wait()
    total = own[...] + pr[1].astype(F32) + pr[3].astype(F32)
    normed, inverse = normalize(xv[...].astype(F32))
    first = jnp.mean(total, axis=-1, keepdims=True)
    second = jnp.mean(total * normed, axis=-1, keepdims=True)
    grads_ref[...] = (
        ctc[core].astype(F32) + (total - first - normed * second) * inverse
    ).astype(BF16)

    wg_column.wait()
    wg_ref[...] = jnp.sum(wzr[...].astype(F32), axis=0)

    finish()


def on_device(inputs, input_weight, output_weight, cotangent, lengths, buckets, bias_weights):
    vm = lambda *shape, dt=BF16: pltpu.VMEM(shape, dt)
    sem = lambda n: pltpu.SemaphoreType.DMA((n,))
    scratch = [
        vm(8, ROWS, D), vm(2, 32, 512), vm(32, D), vm(32, D),
        vm(2, 4, 4, 32, 512), vm(2, 4, 4, 32, D),
        vm(512, D), vm(NBLK, 512, BLK, dt=F32), vm(NBLK, 512, BLK),
        vm(NBLK, BLK, HD), vm(NBLK, BLK, HD),
        vm(PAIRS, BLK, BLK), vm(PAIRS, BLK, BLK, dt=F32), vm(NBLK, BLK, BLK, dt=F32),
        vm(NBLK, HD, BLK, dt=F32), vm(NBLK, HD, BLK, dt=F32),
        vm(4, HD, BLK), vm(4, HD, BLK),
        vm(NBLK, 8, HD, dt=F32), vm(8, NBLK, 8, HD, dt=F32),
        vm(8, HD, ROWS), vm(8, HD, ROWS), vm(8, HD, ROWS), vm(8, HD, ROWS),
        vm(D, ROWS), vm(D, ROWS), vm(2, ROWS, D), vm(ROWS, D), vm(NBLK, HD, BLK),
        vm(NBLK, HD, BLK, dt=F32), vm(NBLK, HD, BLK, dt=F32),
        vm(NBLK, 512, BLK),
        vm(2, PLANE, 32, 512), vm(PLANE, 2, 32, 512),
        vm(8, 32, HD), vm(8, 32, HD),
        vm(NBLK, ROWS, D), vm(NBLK, ROWS, D), vm(NBLK, ROWS, D, dt=F32),
        vm(4, ROWS, D), vm(4, ROWS, D), vm(2, 64, D), vm(ROWS, D, dt=F32),
        sem(8), sem(8), sem(8), sem(8), sem(2), sem(2), sem(64), sem(64), sem(1), sem(1),
        sem(8), sem(8), sem(32), sem(32), sem(8), sem(8),
        sem(2), sem(2), sem(16), sem(16), sem(8), sem(8), sem(4), sem(4), sem(6), sem(6),
        sem(8), sem(8), sem(7),
    ]
    vspec = pl.BlockSpec(memory_space=pltpu.VMEM)
    aspec = pl.BlockSpec(memory_space=pl.ANY)
    sspec = pl.BlockSpec(memory_space=pltpu.SMEM)
    return pl.pallas_call(
        kernel,
        name="hstu",
        out_shape=(
            jax.ShapeDtypeStruct((ROWS, D), BF16),
            jax.ShapeDtypeStruct((ROWS, D), BF16),
            jax.ShapeDtypeStruct((32, HD), F32),
        ),
        in_specs=[sspec, sspec, vspec, aspec, aspec, aspec, aspec],
        out_specs=(vspec, vspec, vspec),
        scratch_shapes=scratch,
        compiler_params=pltpu.CompilerParams(
            collective_id=0, has_side_effects=True, vmem_limit_bytes=56 << 20
        ),
    )(lengths, bias_weights, buckets.reshape(1, SEQ), inputs, input_weight, output_weight, cotangent)


def solution(mesh):
    return jax.shard_map(
        on_device,
        mesh=mesh,
        in_specs=(
            P(("dp", "ctx"), None),
            P("dp", None),
            P("dp", None),
            P(("dp", "ctx"), None),
            P("dp", None),
            P(),
            P(),
        ),
        out_specs=(P(("dp", "ctx"), None), P(("dp", "ctx"), None), P("dp", "ctx")),
        check_vma=False,
    )
```

time: 96.1 us -> 93.7 us (0.975)
  the two profiles are of different devices: /device:TPU:1 before, /device:TPU:4 now
where the time goes in v3:
time: 93.7 us; the launch traced here: 93.5 us
  Pallas kernels  89.8 us (96%)
  local copies, waits for them, and re-layouts  3.04 us (3%)
    pallas_call x1, Pallas kernels, on_device(): pl.pallas_call(kernel, name='hstu', out_shape=(jax.ShapeDtypeStruct((ROWS...  89.8 us
    unnamed x7, local copies, waits for them, and re-layouts  3.04 us

profile of v3, /device:TPU:4, one launch (start us, length us, event | category | flops | bytes accessed | tf_op | source)
XLA Modules:
  0.0 93.5 jit_solution(4998397649018925900)
XLA Ops:
  0.6 89.8 %hstu.1 = (bf16[128,1024]{1,0:T(8,128)(2,1)}, bf16[128,1024]{1,0:T(8,128)(2,1)}, f32[32,128]{1,0:T(8,128)}) custom-call(s32[1,4]{1,0:T(1,128)} %lengths_ref.1, f32[8,32]{1,0:T(8,128)} %bias_ref.1, s32[1,1024]{1,0:T(1,128)} %bitcast.1, bf16[128,1024]{1,0:T(8,128)(2,1)} %x_ref.1, bf16[32,4096]{1,0:T(8,128)(2,1)} %win_ref.1, bf16[32,1024]{1,0:T(8,128)(2,1)} %wout_ref.1, ...), custom_call_target="tpu_custom_call" | custom-call | tf_op jit(solution)/shard_map/hstu/pallas_call | solution.py:642
  90.5 0.0 copy-start
  90.5 1.7 %copy.13 = bf16[128,1024]{1,0:T(8,128)(2,1)} copy(bf16[128,1024]{1,0:T(8,128)(2,1)} %get-tuple-element.6) | data formatting | bytes 524288
  92.2 0.0 copy-done
  92.2 0.0 copy-start.1
  92.2 0.7 copy.14
  92.9 0.0 copy-done.1
  92.9 0.6 copy.15
Async XLA Ops:
  90.5 1.7 %copy-start = (bf16[128,1024]{1,0:T(8,128)(2,1)S(1)}, bf16[128,1024]{1,0:T(8,128)(2,1)}, u32[]{:S(2)}) copy-start(bf16[128,1024]{1,0:T(8,128)(2,1)} %get-tuple-element.7) | copy-start | bytes 786436
  92.2 0.7 copy-start.1

commit v4 on v3

--- a/solution.py
+++ b/solution.py
@@ -52,11 +52,11 @@
     lengths_ref, bias_ref, buckets_ref, x_ref, win_ref, wout_ref, ct_ref,
     out_ref, grads_ref, wg_ref,
     xg, wa, wb, wbo, wra, wrb, wct, pret, actt, krow, vrow, wts, sgs, toep, attt, uf,
-    dgs, dgr, stat, statr, ats, atr, uts, utr, gto, gtm, ctc, xv, dat, dkt, dvt, dpt,
+    dgs, dgr, stat, statr, gstat, gstatr, moments, gts, gtr, gtm, ctc, xv, dat, dkt, dvt, dpt,
     wgs, wgr, wzs, wzr,
     pd, pdr, pm, ps, pr, rr, own,
     xs, xr, xfs, xfr, was, war, wps, wpr, wos, wor, dss, dsr, sts, strr, gss, gsr,
-    wds, wdr, wgss, wgsr, wzss, wzsr, pds, pdsr, pss, psr, uss, usr, lds,
+    wds, wdr, wgss, wgsr, wzss, wzsr, pds, pdsr, pss, psr, lds,
 ):
     dp = lax.axis_index("dp")
     ctx = lax.axis_index("ctx")
@@ -361,12 +361,6 @@
         to_mate_rows[2][h].wait()
     project((zh + 2) % 4)
 
-    for b in range(NBLK):
-        uts[2 * b] = actt[b, 0:HD, 0:ROWS]
-        uts[2 * b + 1] = actt[b, 0:HD, ROWS:]
-    u_sent = all_to_all(uts, utr, uss, usr).start()
-    utr[ctx] = uts[ctx]
-
     l0, l1, l2 = lengths_ref[0, 0], lengths_ref[0, 1], lengths_ref[0, 2]
     e0, e1, e2 = l0, l0 + l1, l0 + l1 + l2
 
@@ -389,47 +383,74 @@
             att = att + nn(actt[j, HD:2 * HD, :], weights)
         attt[i] = att
 
-    def statistics(b):
+    def packed(ref, pieces):
+        for n in range(2):
+            rows = []
+            for b in (2 * n, 2 * n + 1):
+                rows += [q[:, :ROWS] for q in pieces[b]] + [q[:, ROWS:] for q in pieces[b]]
+            ref[n] = jnp.concatenate(rows, axis=0)
+
+    def unpacked(ref, r, b):
+        q = ref[r, b // 2, (b % 2) * 4:(b % 2) * 4 + 4]
+        return (
+            jnp.concatenate([q[0:1], q[2:3]], axis=1), jnp.concatenate([q[1:2], q[3:4]], axis=1)
+        )
+
+    def to_group(src, dst, base):
+        return Copies(lambda t, landed: (
+            src, dst.at[from_ctx(t) if landed else ctx], sts.at[base + t], strr.at[base + t],
+            (dp, ctx_peer(t))), 1, 8).start()
+
+    for b in (3, 2, 1, 0):
+        forward(b)
+    pieces = []
+    for b in range(NBLK):
         att = attt[b]
-        up = dgr[b].astype(F32) * actt[b, 0:HD, :].astype(F32)
         mean = jnp.sum(att, axis=0, keepdims=True) * (1.0 / HD)
         cen = att - mean
-        ats[2 * b] = cen[:, 0:ROWS].astype(BF16)
-        ats[2 * b + 1] = cen[:, ROWS:].astype(BF16)
-        rows = [
-            mean,
-            jnp.sum(cen * cen, axis=0, keepdims=True),
-            jnp.sum(up, axis=0, keepdims=True),
-            jnp.sum(up * cen, axis=0, keepdims=True),
-        ]
-        stat[b] = jnp.concatenate([q[:, :ROWS] for q in rows] + [q[:, ROWS:] for q in rows], axis=0)
-
-    for b in (3, 2, 1, 0):
-        forward(b)
+        pieces.append((mean, jnp.sum(cen * cen, axis=0, keepdims=True)))
+    packed(stat, pieces)
+    att_stats = to_group(stat, statr, 0)
+    statr[ctx] = stat[...]
+
     dg_sent.wait()
-    for b in (3, 2, 1, 0):
-        statistics(b)
-    stats_sent = Copies(lambda t, landed: (
-        stat, statr.at[from_ctx(t) if landed else ctx], sts.at[t], strr.at[t], (dp, ctx_peer(t))), 1, 8).start()
-    statr[ctx] = stat[...]
-    att_sent = all_to_all(ats, atr, gss, gsr).start()
-    atr[ctx] = ats[ctx]
+    grads = []
+    for b in range(NBLK):
+        cen = attt[b] - pieces[b][0]
+        up = dgr[b].astype(F32) * actt[b, 0:HD, :].astype(F32)
+        grads.append((jnp.sum(up, axis=0, keepdims=True), jnp.sum(up * cen, axis=0, keepdims=True)))
+    packed(gstat, grads)
+    grad_stats = to_group(gstat, gstatr, 8)
+    gstatr[ctx] = gstat[...]
+
+    att_stats.wait()
+    for b in range(NBLK):
+        heads = [unpacked(statr, r, b) for r in range(HEADS)]
+        mean = sum([m for m, _ in heads]) * (1.0 / HEADS)
+        var = 0.0
+        for m, v in heads:
+            var = var + v + HD * (m - mean) * (m - mean)
+        inv = lax.rsqrt(var * (1.0 / D) + EPSILON)
+        norm = (attt[b] - mean) * inv
+        attt[b] = norm
+        moments[b, 0:1] = mean
+        moments[b, 1:2] = inv
+        gated = (norm * actt[b, 0:HD, :].astype(F32)).astype(BF16)
+        gts[2 * b] = gated[:, 0:ROWS]
+        gts[2 * b + 1] = gated[:, ROWS:]
+    gated_sent = all_to_all(gts, gtr, gss, gsr).start()
+    gtr[ctx] = gts[ctx]
 
     def combined(b):
-        parts = [
-            jnp.concatenate([statr[r, b, 0:4], statr[r, b, 4:8]], axis=1) for r in range(HEADS)
-        ]
-        mean = sum([q[0:1] for q in parts]) * (1.0 / HEADS)
-        var, s3, s4 = 0.0, 0.0, 0.0
-        for q in parts:
-            off = q[0:1] - mean
-            var = var + q[1:2] + HD * off * off
-            s3 = s3 + q[2:3]
-            s4 = s4 + q[3:4] + off * q[2:3]
-        inv = lax.rsqrt(var * (1.0 / D) + EPSILON)
+        mean, inv = moments[b, 0:1], moments[b, 1:2]
+        s3, s4 = 0.0, 0.0
+        for r in range(HEADS):
+            p, q = unpacked(gstatr, r, b)
+            s3 = s3 + p
+            s4 = s4 + q + (unpacked(statr, r, b)[0] - mean) * p
         m1 = s3 * (1.0 / D)
         m2 = s4 * inv * (1.0 / D)
-        norm = (attt[b] - mean) * inv
+        norm = attt[b]
         dg = dgr[b].astype(F32)
         u = actt[b, 0:HD, :].astype(F32)
         dat[b] = ((dg * u - m1 - norm * m2) * inv).astype(BF16)
@@ -519,46 +540,34 @@
                 ).astype(BF16)
                 near[way, h].go()
 
-    stats_sent.wait()
+    def ct_cols(which):
+        return jnp.concatenate(
+            [ctc[which, :, pl.ds(pl.multiple_of(b * BLK + core * HD, HD), HD)] for b in range(NBLK)], axis=1
+        )
+
+    grad_stats.wait()
     combined(3)
     backward(3)
     terms(3)
-
-    u_sent.wait()
-    att_sent.wait()
-    mine = [jnp.where(core == 0, statr[r, zh, 0:4], statr[r, zh, 4:8]) for r in range(HEADS)]
-    mean = sum([q[0:1] for q in mine]) * (1.0 / HEADS)
-    var = 0.0
-    for q in mine:
-        off = q[0:1] - mean
-        var = var + q[1:2] + HD * off * off
-    inv = lax.rsqrt(var * (1.0 / D) + EPSILON)
-    for r in range(HEADS):
-        norm = (atr[r].astype(F32) + (mine[r][0:1] - mean)) * inv
-        gto[r * HD:(r + 1) * HD] = (norm * utr[r].astype(F32)).astype(BF16)
-    gated_mate = Copies(lambda t, landed: (gto, gtm, wds.at[1], wdr.at[1], mate)).start()
     combined(2)
     backward(2)
     chip_sum(3)
     terms(2)
 
-    def ct_cols(which):
-        return jnp.concatenate(
-            [ctc[which, :, pl.ds(pl.multiple_of(b * BLK + core * HD, HD), HD)] for b in range(NBLK)], axis=1
-        )
-
+    gated_sent.wait()
+    gated_mate = Copies(lambda t, landed: (gtr, gtm, wds.at[1], wdr.at[1], mate)).start()
+    combined(1)
+    backward(1)
+    chip_sum(2)
+    terms(1)
     gated_mate.wait()
-    both = jnp.concatenate([gto[...], gtm[...]], axis=1)
+    both = jnp.concatenate([gtr[...].reshape(D, ROWS), gtm[...].reshape(D, ROWS)], axis=1)
     cts = jnp.concatenate([ct_cols(core), ct_cols(1 - core)], axis=0)
     wgs[...] = nn(both, cts).astype(BF16).reshape(2, PLANE, 32, 512)
     wg_plane = Copies(lambda t, landed: (
         wgs.at[:, plane_peer(t)], wgr.at[plane_from(t) if landed else yx], wgss.at[t], wgsr.at[t],
         (zl * PLANE + plane_peer(t), ctx)), 1, PLANE).start()
     wgr[yx] = wgs[:, yx]
-    combined(1)
-    backward(1)
-    chip_sum(2)
-    terms(1)
     combined(0)
     backward(0)
     chip_sum(1)
@@ -567,7 +576,7 @@
     for b in (3, 2, 1, 0):
         relay(b)
     mates_half.wait()
-    gated = gto[...]
+    gated = gtr[...].reshape(D, ROWS)
     out_ref[...] = (
         xv[...].astype(F32)
         + tn(gated[0:512], wrb[0].reshape(512, D)) + tn(gated[512:], wrb[1].reshape(512, D))
@@ -622,9 +631,9 @@
         vm(PAIRS, BLK, BLK), vm(PAIRS, BLK, BLK, dt=F32), vm(NBLK, BLK, BLK, dt=F32),
         vm(NBLK, HD, BLK, dt=F32), vm(NBLK, HD, BLK, dt=F32),
         vm(4, HD, BLK), vm(4, HD, BLK),
-        vm(NBLK, 8, HD, dt=F32), vm(8, NBLK, 8, HD, dt=F32),
-        vm(8, HD, ROWS), vm(8, HD, ROWS), vm(8, HD, ROWS), vm(8, HD, ROWS),
-        vm(D, ROWS), vm(D, ROWS), vm(2, ROWS, D), vm(ROWS, D), vm(NBLK, HD, BLK),
+        vm(2, 8, HD, dt=F32), vm(8, 2, 8, HD, dt=F32), vm(2, 8, HD, dt=F32), vm(8, 2, 8, HD, dt=F32),
+        vm(NBLK, 8, BLK, dt=F32),
+        vm(8, HD, ROWS), vm(8, HD, ROWS), vm(8, HD, ROWS), vm(2, ROWS, D), vm(ROWS, D), vm(NBLK, HD, BLK),
         vm(NBLK, HD, BLK, dt=F32), vm(NBLK, HD, BLK, dt=F32),
         vm(NBLK, 512, BLK),
         vm(2, PLANE, 32, 512), vm(PLANE, 2, 32, 512),
@@ -634,7 +643,7 @@
         sem(8), sem(8), sem(8), sem(8), sem(2), sem(2), sem(64), sem(64), sem(1), sem(1),
         sem(8), sem(8), sem(32), sem(32), sem(8), sem(8),
         sem(2), sem(2), sem(16), sem(16), sem(8), sem(8), sem(4), sem(4), sem(6), sem(6),
-        sem(8), sem(8), sem(7),
+        sem(7),
     ]
     vspec = pl.BlockSpec(memory_space=pltpu.VMEM)
     aspec = pl.BlockSpec(memory_space=pl.ANY)

time: 93.7 us -> 88.6 us (0.946)
  the two profiles are of different devices: /device:TPU:4 before, /device:TPU:1 now
where the time goes in v4:
time: 88.6 us; the launch traced here: 88.4 us
  Pallas kernels  84.7 us (96%)
  local copies, waits for them, and re-layouts  3.04 us (3%)
    pallas_call x1, Pallas kernels, on_device(): pl.pallas_call(kernel, name='hstu', out_shape=(jax.ShapeDtypeStruct((ROWS...  84.7 us
    unnamed x7, local copies, waits for them, and re-layouts  3.04 us

profile of v4, /device:TPU:1, one launch (start us, length us, event | category | flops | bytes accessed | tf_op | source)
XLA Modules:
  0.0 88.4 jit_solution(10861071832859339093)
XLA Ops:
  0.6 84.7 %hstu.1 = (bf16[128,1024]{1,0:T(8,128)(2,1)}, bf16[128,1024]{1,0:T(8,128)(2,1)}, f32[32,128]{1,0:T(8,128)}) custom-call(s32[1,4]{1,0:T(1,128)} %lengths_ref.1, f32[8,32]{1,0:T(8,128)} %bias_ref.1, s32[1,1024]{1,0:T(1,128)} %bitcast.1, bf16[128,1024]{1,0:T(8,128)(2,1)} %x_ref.1, bf16[32,4096]{1,0:T(8,128)(2,1)} %win_ref.1, bf16[32,1024]{1,0:T(8,128)(2,1)} %wout_ref.1, ...), custom_call_target="tpu_custom_call" | custom-call | tf_op jit(solution)/shard_map/hstu/pallas_call | solution.py:651
  85.3 0.0 copy-start
  85.3 1.7 %copy.13 = bf16[128,1024]{1,0:T(8,128)(2,1)} copy(bf16[128,1024]{1,0:T(8,128)(2,1)} %get-tuple-element.6) | data formatting | bytes 524288
  87.0 0.0 copy-done
  87.0 0.0 copy-start.1
  87.0 0.7 copy.14
  87.7 0.0 copy-done.1
  87.7 0.6 copy.15
Async XLA Ops:
  85.3 1.7 %copy-start = (bf16[128,1024]{1,0:T(8,128)(2,1)S(1)}, bf16[128,1024]{1,0:T(8,128)(2,1)}, u32[]{:S(2)}) copy-start(bf16[128,1024]{1,0:T(8,128)(2,1)} %get-tuple-element.7) | copy-start | bytes 786436
  87.0 0.7 copy-start.1

commit v5 on v4

--- a/solution.py
+++ b/solution.py
@@ -117,12 +117,16 @@
         def sent(self):
             self.each(lambda c: c.wait_send())
 
+    def settle(later=()):
+        for c in [c for c in started if c not in later]:
+            c.sent()
+            started.remove(c)
+
     def finish():
         for c in started:
             if not c.received:
                 c.wait()
-        for c in started:
-            c.sent()
+        settle()
 
     barrier = pltpu.get_barrier_semaphore()
 
@@ -167,6 +171,15 @@
     xg[ctx] = normed.astype(BF16)
     for c in load_w:
         c.wait()
+
+    buckets = buckets_ref[...]
+    table = jnp.zeros((1, SEQ), F32)
+    for b in range(32):
+        table = jnp.where(buckets == b, bias_ref[ctx, b], table)
+    padded = jnp.concatenate([table[:, 0:BLK], table], axis=1)
+    for d in range(NBLK):
+        wide = jnp.broadcast_to(padded[:, d * BLK:d * BLK + 2 * BLK], (BLK, 2 * BLK))
+        toep[d] = pltpu.roll(wide, 0, 1, stride=1, stride_axis=0)[:, BLK:]
 
     pl.semaphore_wait(barrier, 26)
 
@@ -285,28 +298,18 @@
     for w in out_spread:
         w.hand_on()
 
-    buckets = buckets_ref[...]
-    table = jnp.zeros((1, SEQ), F32)
-    for b in range(32):
-        table = jnp.where(buckets == b, bias_ref[ctx, b], table)
-    padded = jnp.concatenate([table[:, 0:BLK], table], axis=1)
-    for d in range(NBLK):
-        wide = jnp.broadcast_to(padded[:, d * BLK:d * BLK + 2 * BLK], (BLK, 2 * BLK))
-        toep[d] = pltpu.roll(wide, 0, 1, stride=1, stride_axis=0)[:, BLK:]
-
     up0.wait()
     far0 = relayed_rows(1, 0).start()
     to_mate_rows[1][0] = mate_rows(1, 0).start()
     down1.wait()
     far1 = relayed_rows(3, 1).start()
     to_mate_rows[3][1] = mate_rows(3, 1).start()
+    for w in in_spread:
+        w.hand_on()
     up1.wait()
     to_mate_rows[1][1] = mate_rows(1, 1).start()
     down0.wait()
     to_mate_rows[3][0] = mate_rows(3, 0).start()
-
-    for w in in_spread:
-        w.hand_on()
 
     for w in out_spread:
         w.wait()
@@ -330,9 +333,6 @@
     @pl.when(from_half == core)
     def _():
         dgr[zh] = dgs[ctx % 4]
-
-    mates_half = Copies(lambda t, landed: (
-        wrb.at[core], wrb.at[1 - core if landed else core], wos.at[0], wor.at[0], mate)).start()
 
     for w in in_spread:
         w.wait()
@@ -440,6 +440,9 @@
         gts[2 * b + 1] = gated[:, ROWS:]
     gated_sent = all_to_all(gts, gtr, gss, gsr).start()
     gtr[ctx] = gts[ctx]
+    mates_half = Copies(lambda t, landed: (
+        wrb.at[core], wrb.at[1 - core if landed else core], wos.at[0], wor.at[0], mate)).start()
+
 
     def combined(b):
         mean, inv = moments[b, 0:1], moments[b, 1:2]
@@ -554,12 +557,16 @@
     chip_sum(3)
     terms(2)
 
-    gated_sent.wait()
-    gated_mate = Copies(lambda t, landed: (gtr, gtm, wds.at[1], wdr.at[1], mate)).start()
     combined(1)
     backward(1)
     chip_sum(2)
     terms(1)
+    gated_sent.wait()
+    gated_mate = Copies(lambda t, landed: (gtr, gtm, wds.at[1], wdr.at[1], mate)).start()
+    combined(0)
+    backward(0)
+    chip_sum(1)
+    terms(0)
     gated_mate.wait()
     both = jnp.concatenate([gtr[...].reshape(D, ROWS), gtm[...].reshape(D, ROWS)], axis=1)
     cts = jnp.concatenate([ct_cols(core), ct_cols(1 - core)], axis=0)
@@ -568,10 +575,6 @@
         wgs.at[:, plane_peer(t)], wgr.at[plane_from(t) if landed else yx], wgss.at[t], wgsr.at[t],
         (zl * PLANE + plane_peer(t), ctx)), 1, PLANE).start()
     wgr[yx] = wgs[:, yx]
-    combined(0)
-    backward(0)
-    chip_sum(1)
-    terms(0)
     chip_sum(0)
     for b in (3, 2, 1, 0):
         relay(b)
@@ -582,6 +585,7 @@
         + tn(gated[0:512], wrb[0].reshape(512, D)) + tn(gated[512:], wrb[1].reshape(512, D))
     ).astype(BF16)
 
+    settle([*far, *near.values(), wg_plane])
     wg_plane.wait()
 
     def add_plane(t, total):
@@ -603,6 +607,8 @@
 
     wg_column = Copies(column, 1, 8).start()
     wzr[zat] = wzs[zat]
+
+    settle([*near.values(), wg_column])
 
     for c in near.values():
         c.wait()
@@ -614,6 +620,7 @@
         ctc[core].astype(F32) + (total - first - normed * second) * inverse
     ).astype(BF16)
 
+    settle([wg_column])
     wg_column.wait()
     wg_ref[...] = jnp.sum(wzr[...].astype(F32), axis=0)
 

time: 88.6 us -> 87.3 us (0.985)
  Pallas kernels: 84.7 us -> 83.4 us
    pallas_call x1, Pallas kernels: 84.7 us -> 83.4 us  [on_device(): pl.pallas_call(kernel, name='hstu', out_shape=(jax.ShapeDtypeStruct((ROWS...]
where the time goes in v5:
time: 87.3 us; the launch traced here: 87.1 us
  Pallas kernels  83.4 us (96%)
  local copies, waits for them, and re-layouts  3.04 us (3%)
    pallas_call x1, Pallas kernels, on_device(): pl.pallas_call(kernel, name='hstu', out_shape=(jax.ShapeDtypeStruct((ROWS...  83.4 us
    unnamed x7, local copies, waits for them, and re-layouts  3.04 us

profile of v5, /device:TPU:1, one launch (start us, length us, event | category | flops | bytes accessed | tf_op | source)
XLA Modules:
  0.0 87.1 jit_solution(2347686330366979686)
XLA Ops:
  0.6 83.4 %hstu.1 = (bf16[128,1024]{1,0:T(8,128)(2,1)}, bf16[128,1024]{1,0:T(8,128)(2,1)}, f32[32,128]{1,0:T(8,128)}) custom-call(s32[1,4]{1,0:T(1,128)} %lengths_ref.1, f32[8,32]{1,0:T(8,128)} %bias_ref.1, s32[1,1024]{1,0:T(1,128)} %bitcast.1, bf16[128,1024]{1,0:T(8,128)(2,1)} %x_ref.1, bf16[32,4096]{1,0:T(8,128)(2,1)} %win_ref.1, bf16[32,1024]{1,0:T(8,128)(2,1)} %wout_ref.1, ...), custom_call_target="tpu_custom_call" | custom-call | tf_op jit(solution)/shard_map/hstu/pallas_call | solution.py:658
  84.0 0.0 copy-start
  84.0 1.7 %copy.13 = bf16[128,1024]{1,0:T(8,128)(2,1)} copy(bf16[128,1024]{1,0:T(8,128)(2,1)} %get-tuple-element.6) | data formatting | bytes 524288
  85.8 0.0 copy-done
  85.8 0.0 copy-start.1
  85.8 0.7 copy.14
  86.5 0.0 copy-done.1
  86.5 0.6 copy.15
Async XLA Ops:
  84.0 1.7 %copy-start = (bf16[128,1024]{1,0:T(8,128)(2,1)S(1)}, bf16[128,1024]{1,0:T(8,128)(2,1)}, u32[]{:S(2)}) copy-start(bf16[128,1024]{1,0:T(8,128)(2,1)} %get-tuple-element.7) | copy-start | bytes 786436
  85.8 0.7 copy-start.1

commit v6 on v5

--- a/solution.py
+++ b/solution.py
@@ -223,23 +223,26 @@
             self.cross = "y" if axis == "x" else "x"
             self.first, self.rest = [], []
 
-        def own(self):
+        def own(self, part=None, k=0):
+            src = self.src if part is None else self.src.at[part]
             for axis in (self.axis, self.cross):
                 for t in (1, 3, 2):
-                    at = self.base + (axis == self.cross) * 3 + t - 1
+                    at = self.base + 6 * k + (axis == self.cross) * 3 + t - 1
 
                     def make(_, landed, axis=axis, t=t, at=at):
                         py, px = step_by(axis, y, x, 4 - t) if landed else (y, x)
-                        return (self.src, self.dst(py, px), wps.at[at], wpr.at[at],
+                        dst = self.dst(py, px)
+                        return (src, dst if part is None else dst.at[part], wps.at[at], wpr.at[at],
                                 in_plane(step_by(axis, y, x, t)))
 
                     (self.first if axis == self.axis else self.rest).append(Copies(make).start())
 
         def hand_on(self):
             for n, t in enumerate((1, 3, 2)):
-                self.first[n].wait()
+                for c in self.first[n::3]:
+                    c.wait()
                 for u in (1, 3, 2):
-                    at = self.base + 6 + (t - 1) * 3 + u - 1
+                    at = self.base + 12 + (t - 1) * 3 + u - 1
 
                     def make(_, landed, t=t, u=u, at=at):
                         py, px = step_by(self.axis, y, x, 4 - t)
@@ -274,11 +277,18 @@
     def _():
         wb[...] = wbo[...]
 
+    low, high = pl.ds(0, 256), pl.ds(256, 256)
+    in_spread = [
+        Spread(wa.at[:, :, low], lambda py, px: wra.at[:, py, px, :, low], "x", 48),
+        Spread(wa.at[:, :, high], lambda py, px: wra.at[:, py, px, :, high], "y", 72),
+    ]
+    for w in in_spread:
+        w.own(pl.ds(zl, 1), 0)
     xb.wait()
     lo, hi = pl.ds(0, 512), pl.ds(512, 512)
     out_spread = [
         Spread(wb.at[:, lo], lambda py, px: wrb.at[core, py, px, :, lo], "x", 0),
-        Spread(wb.at[:, hi], lambda py, px: wrb.at[core, py, px, :, hi], "y", 16),
+        Spread(wb.at[:, hi], lambda py, px: wrb.at[core, py, px, :, hi], "y", 24),
     ]
     for w in out_spread:
         w.own()
@@ -286,13 +296,8 @@
     ct_mate = Copies(lambda t, landed: (
         ctc.at[core], ctc.at[1 - core if landed else core], wds.at[0], wdr.at[0], mate)).start()
     xa.wait()
-    low, high = pl.ds(0, 256), pl.ds(256, 256)
-    in_spread = [
-        Spread(wa.at[:, :, low], lambda py, px: wra.at[:, py, px, :, low], "x", 32),
-        Spread(wa.at[:, :, high], lambda py, px: wra.at[:, py, px, :, high], "y", 48),
-    ]
     for w in in_spread:
-        w.own()
+        w.own(pl.ds(1 - zl, 1), 1)
     wrb[core, y, x] = wb[...]
     wra[:, y, x] = wa[...]
     for w in out_spread:
@@ -560,13 +565,12 @@
     combined(1)
     backward(1)
     chip_sum(2)
-    terms(1)
     gated_sent.wait()
     gated_mate = Copies(lambda t, landed: (gtr, gtm, wds.at[1], wdr.at[1], mate)).start()
+    terms(1)
     combined(0)
     backward(0)
     chip_sum(1)
-    terms(0)
     gated_mate.wait()
     both = jnp.concatenate([gtr[...].reshape(D, ROWS), gtm[...].reshape(D, ROWS)], axis=1)
     cts = jnp.concatenate([ct_cols(core), ct_cols(1 - core)], axis=0)
@@ -575,6 +579,7 @@
         wgs.at[:, plane_peer(t)], wgr.at[plane_from(t) if landed else yx], wgss.at[t], wgsr.at[t],
         (zl * PLANE + plane_peer(t), ctx)), 1, PLANE).start()
     wgr[yx] = wgs[:, yx]
+    terms(0)
     chip_sum(0)
     for b in (3, 2, 1, 0):
         relay(b)
@@ -647,7 +652,7 @@
         vm(8, 32, HD), vm(8, 32, HD),
         vm(NBLK, ROWS, D), vm(NBLK, ROWS, D), vm(NBLK, ROWS, D, dt=F32),
         vm(4, ROWS, D), vm(4, ROWS, D), vm(2, 64, D), vm(ROWS, D, dt=F32),
-        sem(8), sem(8), sem(8), sem(8), sem(2), sem(2), sem(64), sem(64), sem(1), sem(1),
+        sem(8), sem(8), sem(8), sem(8), sem(2), sem(2), sem(96), sem(96), sem(1), sem(1),
         sem(8), sem(8), sem(32), sem(32), sem(8), sem(8),
         sem(2), sem(2), sem(16), sem(16), sem(8), sem(8), sem(4), sem(4), sem(6), sem(6),
         sem(7),

time: 87.3 us -> 86.5 us (level)
  no operation moved by 1% of the time
where the time goes in v6:
time: 86.5 us; the launch traced here: 86.3 us
  Pallas kernels  82.7 us (96%)
  local copies, waits for them, and re-layouts  3.04 us (4%)
    pallas_call x1, Pallas kernels, on_device(): pl.pallas_call(kernel, name='hstu', out_shape=(jax.ShapeDtypeStruct((ROWS...  82.7 us
    unnamed x7, local copies, waits for them, and re-layouts  3.04 us

profile of v6, /device:TPU:1, one launch (start us, length us, event | category | flops | bytes accessed | tf_op | source)
XLA Modules:
  0.0 86.3 jit_solution(2036568191326777344)
XLA Ops:
  0.6 82.7 %hstu.1 = (bf16[128,1024]{1,0:T(8,128)(2,1)}, bf16[128,1024]{1,0:T(8,128)(2,1)}, f32[32,128]{1,0:T(8,128)}) custom-call(s32[1,4]{1,0:T(1,128)} %lengths_ref.1, f32[8,32]{1,0:T(8,128)} %bias_ref.1, s32[1,1024]{1,0:T(1,128)} %bitcast.1, bf16[128,1024]{1,0:T(8,128)(2,1)} %x_ref.1, bf16[32,4096]{1,0:T(8,128)(2,1)} %win_ref.1, bf16[32,1024]{1,0:T(8,128)(2,1)} %wout_ref.1, ...), custom_call_target="tpu_custom_call" | custom-call | tf_op jit(solution)/shard_map/hstu/pallas_call | solution.py:663
  83.3 0.0 copy-start
  83.3 1.7 %copy.13 = bf16[128,1024]{1,0:T(8,128)(2,1)} copy(bf16[128,1024]{1,0:T(8,128)(2,1)} %get-tuple-element.6) | data formatting | bytes 524288
  85.0 0.0 copy-done
  85.0 0.0 copy-start.1
  85.0 0.7 copy.14
  85.7 0.0 copy-done.1
  85.7 0.6 copy.15
Async XLA Ops:
  83.3 1.7 %copy-start = (bf16[128,1024]{1,0:T(8,128)(2,1)S(1)}, bf16[128,1024]{1,0:T(8,128)(2,1)}, u32[]{:S(2)}) copy-start(bf16[128,1024]{1,0:T(8,128)(2,1)} %get-tuple-element.7) | copy-start | bytes 786436
  85.0 0.7 copy-start.1
